TPU v7x, 32 devices: a whole 2x2x4 slice. The times are simulated.
32 devices in a mesh: vis: 2 (over x), grp: 8 (over z, core), enc: 2 (over y).
Axes of the slice: x: 2, y: 2, z: 4, core: 2. Of those that a mesh axis runs over, the one named last changes fastest.
Arguments:
- image_tokens: bfloat16 [8, 256, 6144], P('grp', None, 'enc'), may hold values from -8 to 8
- vision_gain: float32 [6144], P('enc'), may hold values from 0.1 to 1.9
- up_weight: bfloat16 [6144, 12288], P('enc', ('vis', 'grp')), may hold values from -0.078125 to 0.078125
- down_weight: bfloat16 [12288, 6144], P(('vis', 'grp'), 'enc'), may hold values from -0.0546875 to 0.0546875
- project_weight: bfloat16 [6144, 4096], P('enc', 'vis'), may hold values from -0.078125 to 0.078125
- encoder_gain: float32 [4096], P('vis'), may hold values from 0.1 to 1.9
- qkv_weight: bfloat16 [3, 4096, 2048], P(None, 'vis', 'enc'), may hold values from -0.6 to 0.6
- out_weight: bfloat16 [2048, 4096], P('enc', 'vis'), may hold values from -0.5 to 0.5
- captions: bfloat16 [32, 16, 4096], P('grp', 'enc', 'vis'), may hold values from -8 to 8
- cand_counts: int32 [8], replicated, may hold values from 1 to 12, 32 in all
- caption_lengths: int32 [32], P('grp'), may hold values from 1 to 16
Outputs:
- vision_out: bfloat16 [8, 256, 6144], P('grp', None, 'enc')
- caption_out: bfloat16 [32, 16, 4096], P('grp', 'enc', 'vis')
Inputs may be any that keep to these rules, and one draw needn't show every extreme that they name: `cand_counts`: every image has at least one candidate, the counts sum to 32 and the largest is 12.
All inputs are finite; a program needn't handle non-finite values.
Results may differ from a plain program's by a relative error of at most 0.035.
Values may be sent and summed in bfloat16 or wider, within the bound.
No kernel may reach another device: no remote copies, remote signals or barrier semaphores. Data moves between devices by JAX's collectives and lax.ppermute only.
A program may use at most 192 MiB of HBM per device.

v0:
```python
import jax
import jax.numpy as jnp
from jax import lax
from jax.sharding import PartitionSpec as P

D = 6144
R = 256
DE = 4096
DH = 256
CAP = 16


EPSILON = 1e-06
FLOOR = -1e30


def image_of(counts, candidate):
    ends = jnp.cumsum(counts)
    return jnp.sum((candidate[:, None] >= ends[None, :]).astype(jnp.int32), axis=1)


def softmax_update(state, query, keys, values, allowed):
    top, total, accum = state
    heads = query.shape[1]
    width = query.shape[2]
    count = keys.shape[0]
    key_heads = keys.reshape(count, heads, width)
    value_heads = values.reshape(count, heads, width)
    scores = jnp.einsum(
        "qhd,khd->qhk", query, key_heads, preferred_element_type=jnp.float32
    ) * width ** (-0.5)
    scores = jnp.where(allowed[:, None, :], scores, FLOOR)
    new_top = jnp.maximum(top, jnp.max(scores, axis=-1))
    weights = jnp.where(allowed[:, None, :], jnp.exp(scores - new_top[..., None]), 0.0)
    factor = jnp.exp(top - new_top)
    total = total * factor + jnp.sum(weights, axis=-1)
    accum = accum * factor[..., None] + jnp.einsum(
        "qhk,khd->qhd",
        weights.astype(jnp.bfloat16),
        value_heads,
        preferred_element_type=jnp.float32,
    )
    return (new_top, total, accum)


def on_device(
    image_tokens,
    vision_gain,
    up_weight,
    down_weight,
    project_weight,
    encoder_gain,
    qkv_weight,
    out_weight,
    captions,
    cand_counts,
    caption_lengths,
):
    tokens = image_tokens[0].astype(jnp.float32)
    row_total, row_squares = lax.psum(
        (jnp.sum(tokens, axis=-1), jnp.sum(tokens * tokens, axis=-1)), "enc"
    )
    mean = row_total / D
    spread = row_squares / D - mean * mean
    normed = ((tokens - mean[:, None]) * lax.rsqrt(spread + EPSILON)[:, None] * vision_gain).astype(
        jnp.bfloat16
    )
    partial_pre = jnp.dot(
        normed,
        lax.all_gather(up_weight, "grp", axis=1, tiled=True),
        preferred_element_type=jnp.float32,
    )
    hidden = jax.nn.gelu(lax.psum(partial_pre, "enc"), approximate=False).astype(jnp.bfloat16)
    partial_out = jnp.dot(
        hidden,
        lax.all_gather(down_weight, "grp", axis=0, tiled=True),
        preferred_element_type=jnp.float32,
    )
    vision_rows = (tokens + lax.psum(partial_out, "vis")).astype(jnp.bfloat16)
    embedded = lax.psum(
        jnp.dot(vision_rows, project_weight, preferred_element_type=jnp.float32), "enc"
    )
    words = captions.astype(jnp.float32)
    image_power, word_power = lax.psum(
        (jnp.sum(embedded * embedded, axis=-1), jnp.sum(words * words, axis=-1)), "vis"
    )
    image_normed = (
        embedded * lax.rsqrt(image_power / DE + EPSILON)[:, None] * encoder_gain
    ).astype(jnp.bfloat16)
    word_normed = (words * lax.rsqrt(word_power / DE + EPSILON)[..., None] * encoder_gain).astype(
        jnp.bfloat16
    )
    inner = qkv_weight.shape[2]
    heads = inner // DH
    groups = lax.axis_size("grp")
    vis_count = lax.axis_size("vis")
    gathered = lax.all_gather(word_normed, "enc", axis=1, tiled=True)
    cand_local = gathered.shape[0]
    flat_words = gathered.reshape(cand_local * CAP, gathered.shape[2])
    query_rows = cand_local * CAP // vis_count
    block = flat_words
    projected = lax.psum_scatter(
        jnp.einsum("rd,kdh->rkh", block, qkv_weight, preferred_element_type=jnp.float32),
        "vis",
        scatter_dimension=0,
        tiled=True,
    ).astype(jnp.bfloat16)
    query = projected[:, 0].reshape(query_rows, heads, DH)
    own_rows = lax.all_gather(projected[:, 1:], "vis", axis=0, tiled=True)
    row_ids = lax.axis_index("vis") * query_rows + jnp.arange(query_rows, dtype=jnp.int32)
    query_cand = row_ids // CAP
    query_image = image_of(cand_counts, lax.axis_index("grp") * cand_local + query_cand)
    key_ids = jnp.arange(cand_local * CAP, dtype=jnp.int32)
    key_cand = key_ids // CAP
    key_live = key_ids % CAP < jnp.repeat(caption_lengths, CAP)
    allowed_own = (key_cand[None, :] == query_cand[:, None]) & key_live[None, :]
    initial = (
        jnp.full((query_rows, heads), FLOOR, jnp.float32),
        jnp.zeros((query_rows, heads), jnp.float32),
        jnp.zeros((query_rows, heads, DH), jnp.float32),
    )
    rows_each = R // vis_count
    block = image_normed
    memory = lax.psum_scatter(
        jnp.einsum("rd,kdh->rkh", block, qkv_weight[1:], preferred_element_type=jnp.float32),
        "vis",
        scatter_dimension=0,
        tiled=True,
    ).astype(jnp.bfloat16)
    piece = lax.all_gather(memory, ("vis", "grp"), axis=0, tiled=True)
    sources = jnp.arange(piece.shape[0], dtype=jnp.int32) // rows_each % groups
    allowed = sources[None, :] == query_image[:, None]
    state = softmax_update(initial, query, piece[:, 0], piece[:, 1], allowed)
    state = softmax_update(state, query, own_rows[:, 0], own_rows[:, 1], allowed_own)
    top, total, accum = state
    attended = (accum / total[..., None]).reshape(query_rows, inner).astype(jnp.bfloat16)
    partial_words = jnp.dot(
        lax.all_gather(attended, "vis", axis=0, tiled=True),
        out_weight,
        preferred_element_type=jnp.float32,
    )
    words_out = lax.psum_scatter(
        partial_words.reshape(cand_local, CAP, partial_words.shape[1]),
        "enc",
        scatter_dimension=1,
        tiled=True,
    )
    caption_out = (words + words_out).astype(jnp.bfloat16)
    return (vision_rows[None], caption_out)


def solution(mesh):
    return jax.shard_map(
        on_device,
        mesh=mesh,
        in_specs=(
            P("grp", None, "enc"),
            P("enc"),
            P("enc", ("vis", "grp")),
            P(("vis", "grp"), "enc"),
            P("enc", "vis"),
            P("vis"),
            P(None, "vis", "enc"),
            P("enc", "vis"),
            P("grp", "enc", "vis"),
            P(),
            P("grp"),
        ),
        out_specs=(P("grp", None, "enc"), P("grp", "enc", "vis")),
        check_vma=False,
    )
```

profile of v0, /device:TPU:0, one launch (start us, length us, event | category | flops | bytes accessed | tf_op | source)
XLA Modules:
  0.0 1203.7 jit_solution(13476206900076525780)
XLA Ops:
  7.2 0.7 all-gather.4.cloned.1.call-update
  8.0 0.7 all-gather.6.cloned.1.call-update
  9.4 5.9 all-reduce
  15.3 321.6 %all-gather.4.cloned.1.call-done = bf16[3072,6144]{1,0:T(8,128)(2,1)} async-done(((bf16[3072,768]{1,0:T(8,128)(2,1)}), bf16[3072,6144]{1,0:T(8,128)(2,1)}) %all-gather.4.cloned.1.call-update) | async-done | bytes 37748752 | tf_op jit(solution)/shard_map/all_gather | solution.py:70
  336.9 21.5 %fusion.65 = f32[256,6144]{1,0:T(8,128)} fusion(bf16[3072,6144]{1,0:T(8,128)(2,1)} %all-gather.4.cloned.1.call-done, bf16[1,256,3072]{2,1,0:T(8,128)(2,1)S(1)} %copy-done, f32[3072]{0:T(1024)S(1)} %copy-done.6, f32[256]{0:T(256)S(1)} %get-tuple-element.16, f32[256]{0:T(256)S(1)} %get-tuple-element.15), kind=kOutput, calls=%fused_computation.71 | convolution fusion | flops 9667608576 | bytes 45627392 | tf_op jit(solution)/shard_map/dot_general | solution.py:68
  358.5 303.5 %all-gather.6.cloned.1.call-done = bf16[6144,3072]{1,0:T(8,128)(2,1)} async-done(((bf16[768,3072]{1,0:T(8,128)(2,1)}), bf16[6144,3072]{1,0:T(8,128)(2,1)}) %all-gather.6.cloned.1.call-update) | async-done | bytes 37748752 | tf_op jit(solution)/shard_map/all_gather | solution.py:76
  662.0 154.5 %all-reduce.6.cloned.1.call-done = f32[256,6144]{1,0:T(8,128)} async-done(((f32[256,6144]{1,0:T(8,128)}), f32[256,6144]{1,0:T(8,128)}) %all-reduce.6.cloned.1.call-update) | async-done | bytes 6291472 | tf_op jit(solution)/shard_map/psum | solution.py:73
  816.5 28.8 %fusion.19 = f32[256,3072]{1,0:T(8,128)} fusion(bf16[6144,3072]{1,0:T(8,128)(2,1)} %all-gather.6.cloned.1.call-done, f32[256,6144]{1,0:T(8,128)} %all-reduce.6.cloned.1.call-done), kind=kOutput, calls=%fused_computation.30 | convolution fusion | flops 9765912576 | bytes 47185920 | tf_op jit(solution)/shard_map/dot_general | solution.py:74
  845.6 85.7 %all-reduce.8.cloned.1.call-done = f32[256,3072]{1,0:T(8,128)} async-done(((f32[256,3072]{1,0:T(8,128)}), f32[256,3072]{1,0:T(8,128)}) %all-reduce.8.cloned.1.call-update) | async-done | bytes 3145744 | tf_op jit(solution)/shard_map/psum | solution.py:79
  931.2 10.3 fusion.147
  941.7 62.9 %all-reduce.10.cloned.1.call-done = f32[256,2048]{1,0:T(8,128)} async-done(((f32[256,2048]{1,0:T(8,128)}), f32[256,2048]{1,0:T(8,128)}) %all-reduce.10.cloned.1.call-update) | async-done | bytes 2097168 | tf_op jit(solution)/shard_map/psum | solution.py:80
  1004.6 1.8 multiply_reduce_fusion
  1006.4 4.9 all-reduce.1
  1011.4 7.8 fusion
  1019.4 5.6 all_gather.21
  1025.0 8.1 fusion.154
  1033.2 18.0 %reduce-scatter.4.cloned.1.call-done = f32[128,2,1024]{2,0,1:T(8,128)} async-done(((f32[256,2,1024]{2,0,1:T(8,128)}), f32[128,2,1024]{2,0,1:T(8,128)}) %reduce-scatter.4.cloned.1.call-update) | async-done | bytes 1048592 | tf_op jit(solution)/shard_map/reduce_scatter | solution.py:124
  1051.2 2.1 convert_element_type.56
  1054.1 17.4 %reduce-scatter.6.cloned.1.call-done = f32[32,3,1024]{2,0,1:T(8,128)} async-done(((f32[64,3,1024]{2,0,1:T(8,128)}), f32[32,3,1024]{2,0,1:T(8,128)}) %reduce-scatter.6.cloned.1.call-update) | async-done | bytes 393232 | tf_op jit(solution)/shard_map/reduce_scatter | solution.py:102
  1071.5 1.0 convert_element_type.58
  1072.6 5.9 all_gather.22
  1078.9 70.0 %all-gather.8.cloned.1.call-done = bf16[2048,2,1024]{2,0,1:T(8,128)(2,1)} async-done(((bf16[128,2,1024]{2,0,1:T(8,128)(2,1)}), bf16[2048,2,1024]{2,0,1:T(8,128)(2,1)}) %all-gather.8.cloned.1.call-update) | async-done | bytes 8388624 | tf_op jit(solution)/shard_map/all_gather | solution.py:130
  1148.9 5.9 fusion.150
  1154.8 7.8 reshape_squeeze.15
  1162.6 7.8 reshape_squeeze.17
  1170.5 3.8 fusion.152
  1174.8 0.9 fusion.78
  1176.0 4.9 all_gather.23
  1180.9 1.6 fusion.155
  1182.6 3.5 fusion.149
  1186.0 9.5 reduce-scatter.8.cloned.1.call-done
  1195.5 1.6 fusion.98
  (63 shorter events, 3.5 us)
Async XLA Ops:
  7.2 1.6 copy-start
  7.2 329.7 %copy-start.6 = (f32[3072]{0:T(1024)S(1)}, f32[3072]{0:T(1024)}, u32[]{:S(2)}) copy-start(f32[3072]{0:T(1024)} %param.12) | copy-start | bytes 36868
  7.2 329.7 %all-gather.4.cloned.1.call-start = ((), (), s32[]{:S(2)}) async-start(), calls=%async_computation.3 | async-start | bytes 42467328 | tf_op jit(solution)/shard_map/all_gather | solution.py:70
  7.9 654.1 %all-gather.6.cloned.1.call-start = ((), (), s32[]{:S(2)}) async-start(), calls=%async_computation.5 | async-start | bytes 42467328 | tf_op jit(solution)/shard_map/all_gather | solution.py:76
  8.7 807.8 %all-reduce.6.cloned.1.call-start = ((), (), s32[]{:S(2)}) async-start(), calls=%async_computation.4 | async-start | bytes 12582912 | tf_op jit(solution)/shard_map/psum | solution.py:73
  358.4 572.8 %all-reduce.8.cloned.1.call-start = ((), (), s32[]{:S(2)}) async-start(), calls=%async_computation.6 | async-start | bytes 6291456 | tf_op jit(solution)/shard_map/psum | solution.py:79
  845.3 96.3 %copy-start.3 = (bf16[4,8,2048]{2,1,0:T(8,128)(2,1)S(1)}, bf16[4,8,2048]{2,1,0:T(8,128)(2,1)}, u32[]{:S(2)}) copy-start(bf16[4,8,2048]{2,1,0:T(8,128)(2,1)} %param.19) | copy-start | bytes 393220
  845.3 166.1 %copy-start.4 = (f32[2048]{0:T(1024)S(1)}, f32[2048]{0:T(1024)}, u32[]{:S(2)}) copy-start(f32[2048]{0:T(1024)} %param.16) | copy-start | bytes 24580
  845.3 159.3 %all-reduce.10.cloned.1.call-start = ((), (), s32[]{:S(2)}) async-start(), calls=%async_computation.7 | async-start | bytes 4194304 | tf_op jit(solution)/shard_map/psum | solution.py:80
  941.6 109.6 %reduce-scatter.4.cloned.1.call-start = ((), (), s32[]{:S(2)}) async-start(), calls=%async_computation.8 | async-start | bytes 3145728 | tf_op jit(solution)/shard_map/reduce_scatter | solution.py:124
  1019.2 52.3 %reduce-scatter.6.cloned.1.call-start = ((), (), s32[]{:S(2)}) async-start(), calls=%async_computation.10 | async-start | bytes 1179648 | tf_op jit(solution)/shard_map/reduce_scatter | solution.py:102
  1025.0 28.4 %copy-start.5 = (s32[4]{0:T(128)S(1)}, s32[4]{0:T(128)}, u32[]{:S(2)}) copy-start(s32[4]{0:T(128)} %param.21) | copy-start | bytes 52
  1025.0 28.5 %copy-start.7 = (s32[8]{0:T(128)S(1)}, s32[8]{0:T(128)}, u32[]{:S(2)}) copy-start(s32[8]{0:T(128)} %param.20) | copy-start | bytes 100
  1033.2 115.7 %all-gather.8.cloned.1.call-start = ((), (), s32[]{:S(2)}) async-start(), calls=%async_computation.9 | async-start | bytes 8912896 | tf_op jit(solution)/shard_map/all_gather | solution.py:130
  1053.3 142.2 %reduce-scatter.8.cloned.1.call-start = ((), (), s32[]{:S(2)}) async-start(), calls=%async_computation.11 | async-start | bytes 786432 | tf_op jit(solution)/shard_map/reduce_scatter | solution.py:142
  1170.5 4.3 copy-start.2
  1174.3 6.6 copy-start.1
Sparse Core Ops, SparseCore 0:
  9.6 327.2 all-gather.3
  338.6 323.3 all-gather.5
  664.4 152.0 all-reduce.5
  845.4 85.7 all-reduce.7
  941.7 62.9 all-reduce.9
  1019.3 31.8 reduce-scatter.3
  1054.0 17.4 reduce-scatter.5
  1073.9 74.8 all-gather.7
  1182.7 12.7 reduce-scatter.7
where the time goes:
time: 1200 us
  waiting for transfers between devices  1040 us (87%)
  matrix products  83.2 us (7%)
  blocking collectives  27.3 us (2%)
  local copies, waits for them, and re-layouts  22 us (2%)
  between operations  14 us (1%)
  other arithmetic  12 us (1%)
    all_gather x1, waiting for transfers between devices, on_device(): lax.all_gather(up_weight, 'grp', axis=1, tiled=True)  322 us
    all_gather x1, waiting for transfers between devices, on_device(): lax.all_gather(down_weight, 'grp', axis=0, tiled=True)  304 us
    psum x1, waiting for transfers between devices, on_device(): lax.psum(partial_pre, 'enc')  155 us
    psum x1, waiting for transfers between devices, on_device(): vision_rows = (tokens + lax.psum(partial_out, 'vis')).astype(jnp.bfloat16)  85.7 us
    all_gather x1, waiting for transfers between devices, on_device(): piece = lax.all_gather(memory, ('vis', 'grp'), axis=0, tiled=True)  70 us
    psum x1, waiting for transfers between devices, on_device(): lax.psum(jnp.dot(vision_rows, project_weight, preferred_element_type=jnp....  62.9 us
    dot_general x1, matrix products, on_device(): jnp.dot(hidden, lax.all_gather(down_weight, 'grp', axis=0, tiled=True), p...  28.8 us
  transfers between devices with their start and end apart: 9, of which 9 were waited for; matrix products, arithmetic and copies ran while one was open for 3% of the time, Pallas kernels for 0%

commit v1 on v0

v1 whole, which is shorter than its diff:
```python
import jax
import jax.numpy as jnp
from jax import lax
from jax.sharding import PartitionSpec as P

DH = 256
CAP = 16
MOSTC = 12


EPSILON = 1e-06
FLOOR = -1e30


def image_of(counts, candidate):
    ends = jnp.cumsum(counts)
    return jnp.sum((candidate[:, None] >= ends[None, :]).astype(jnp.int32), axis=1)


def dot(a, b):
    return jnp.dot(a, b, preferred_element_type=jnp.float32)


def wide(a):
    return a.astype(jnp.float32)


def slim(a):
    return a.astype(jnp.bfloat16)


def shifted(value, axis, step):
    count = lax.axis_size(axis)
    return lax.ppermute(value, axis, [(i, (i + step) % count) for i in range(count)])


def summed(value, axis):
    if lax.axis_size(axis) != 2:
        return lax.psum(value, axis)
    return value + shifted(value, axis, 1)


def joined(value, axis, dim):
    if lax.axis_size(axis) != 2:
        return lax.all_gather(value, axis, axis=dim, tiled=True)
    other = shifted(value, axis, 1)
    first = lax.axis_index(axis) == 0
    return jnp.concatenate(
        [jnp.where(first, value, other), jnp.where(first, other, value)], axis=dim
    )


def on_device(
    image_tokens,
    vision_gain,
    up_weight,
    down_weight,
    project_weight,
    encoder_gain,
    qkv_weight,
    out_weight,
    captions,
    cand_counts,
    caption_lengths,
):
    vis_count = lax.axis_size("vis")
    enc_count = lax.axis_size("enc")
    groups = lax.axis_size("grp")
    vis = lax.axis_index("vis")
    group = lax.axis_index("grp")
    rows, features = image_tokens.shape[1:]
    all_features = features * enc_count
    width = captions.shape[2] * vis_count
    pair = vis_count == 2
    part_rows = rows // vis_count

    cores = 2 if groups % 2 == 0 else 1
    places = groups // cores
    up_parts, down_parts = [up_weight], [down_weight]
    if cores == 2:
        swap = [(i, i ^ 1) for i in range(groups)]
        up_parts.append(lax.ppermute(up_weight, "grp", swap))
        down_parts.append(lax.ppermute(down_weight, "grp", swap))

    def to_place(value, step):
        return lax.ppermute(
            value, "grp", [(i, (i + step * cores) % groups) for i in range(groups)]
        )

    def mine_of(value):
        return lax.dynamic_slice_in_dim(value, vis * part_rows, part_rows, axis=0)

    def by_halves(value):
        if not pair:
            return value
        return jnp.concatenate(
            [mine_of(value), lax.dynamic_slice_in_dim(value, (1 - vis) * part_rows, part_rows, axis=0)]
        )

    def all_rows(mine):
        if not pair:
            return lax.all_gather(mine, "vis", axis=0, tiled=True)
        return jnp.concatenate([mine, shifted(mine, "vis", 1)])

    def my_rows_sum(value):
        if not pair:
            return lax.psum_scatter(value, "vis", scatter_dimension=0, tiled=True)
        return value[:part_rows] + wide(shifted(slim(value[part_rows:]), "vis", 1))

    tokens = wide(image_tokens[0])
    row_total, row_squares = summed(
        jnp.stack([jnp.sum(tokens, axis=-1), jnp.sum(tokens * tokens, axis=-1)]), "enc"
    )
    mean = row_total / all_features
    spread = row_squares / all_features - mean * mean
    normed = slim(
        (tokens - mean[:, None]) * lax.rsqrt(spread + EPSILON)[:, None] * vision_gain
    )
    my_normed = mine_of(normed)

    def pre_of(block):
        return [dot(block, weight) for weight in up_parts]

    def out_of(pre):
        total = None
        for part, weight in zip(pre, down_parts):
            if enc_count == 2:
                full = part + wide(shifted(slim(part), "enc", 1))
            else:
                full = lax.psum(part, "enc")
            term = dot(slim(jax.nn.gelu(full, approximate=False)), weight)
            total = term if total is None else total + term
        return total

    order = [0] + list(range(1, places))
    my_out = None
    blocks = [by_halves(normed)]
    blocks += [all_rows(to_place(my_normed, step)) for step in order[1:]]
    for step, block in zip(order, blocks):
        partial = my_rows_sum(out_of(pre_of(block)))
        if step:
            partial = wide(to_place(slim(partial), -step))
        my_out = partial if my_out is None else my_out + partial
    my_vision = slim(mine_of(tokens) + my_out)

    inner = qkv_weight.shape[2]
    heads = inner // DH
    shares = vis_count if heads % vis_count == 0 else 1
    share = inner // shares
    words = wide(captions)
    all_words = wide(joined(captions, "enc", 1))
    word_power = summed(jnp.sum(all_words * all_words, axis=-1), "vis")
    word_normed = slim(
        all_words * lax.rsqrt(word_power / width + EPSILON)[..., None] * encoder_gain
    )
    cand_local = word_normed.shape[0]
    word_rows = cand_local * CAP
    flat_words = word_normed.reshape(word_rows, word_normed.shape[2])

    def head_weights(which):
        return lax.dynamic_slice_in_dim(qkv_weight, which * share, share, axis=2)

    def head_sum(values, scale=None):
        if shares == 1:
            return lax.psum(values, "vis")
        return lax.psum_scatter(values, "vis", scatter_dimension=2, tiled=True)

    if pair and shares == 2:
        my_heads, other_heads = head_weights(vis), head_weights(1 - vis)

        def project_heads(block, first):
            sent = jnp.einsum(
                "rd,kdh->rkh", block, other_heads[first:], preferred_element_type=jnp.float32
            )
            kept = jnp.einsum(
                "rd,kdh->rkh", block, my_heads[first:], preferred_element_type=jnp.float32
            )
            return kept, slim(sent)

        kept, sent = project_heads(flat_words, 0)
        word_qkv = slim(kept + wide(shifted(sent, "vis", 1)))
    else:
        word_qkv = slim(
            head_sum(
                jnp.einsum(
                    "rd,kdh->rkh", flat_words, qkv_weight, preferred_element_type=jnp.float32
                )
            )
        )
    every_word = lax.all_gather(word_qkv, "grp", axis=0, tiled=True)
    every_length = lax.all_gather(wide(caption_lengths), "grp", axis=0, tiled=True)

    def embed(block):
        partial = dot(block, project_weight)
        if enc_count == 2:
            full = partial + wide(shifted(slim(partial), "enc", 1))
        else:
            full = lax.psum(partial, "enc")
        return slim(full * encoder_gain), jnp.sum(full * full, axis=-1)

    if pair and shares == 2:
        other_vision = shifted(my_vision, "vis", 1)
        vision_rows = jnp.where(
            vis == 0,
            jnp.concatenate([my_vision, other_vision]),
            jnp.concatenate([other_vision, my_vision]),
        )
        pieces = []
        for block in (my_vision, other_vision):
            scaled, power = embed(block)
            pieces.append(project_heads(scaled, 1) + (power,))
        image_kv = []
        for here, there in ((0, 1), (1, 0)):
            total = pieces[here][0] + wide(shifted(pieces[there][1], "vis", 1))
            power = pieces[here][2] + shifted(pieces[there][2], "vis", 1)
            image_kv.append(
                slim(total * lax.rsqrt(power / width + EPSILON)[:, None, None])
            )
        image_kv = jnp.concatenate(image_kv)
    else:
        vision_rows = joined(my_vision, "vis", 0)
        scaled, power = embed(vision_rows)
        total = head_sum(
            jnp.einsum(
                "rd,kdh->rkh", scaled, qkv_weight[1:], preferred_element_type=jnp.float32
            )
        )
        power = lax.psum(power, "vis")
        image_kv = slim(total * lax.rsqrt(power / width + EPSILON)[:, None, None])

    cands = every_length.shape[0]
    most = min(MOSTC, cands)
    ends = jnp.cumsum(cand_counts)
    start = jnp.minimum(ends[group] - cand_counts[group], cands - most)
    near = lax.dynamic_slice_in_dim(every_word, start * CAP, most * CAP, axis=0)
    near = near.reshape(most * CAP, 3, share // DH, DH)
    lengths = lax.dynamic_slice_in_dim(every_length, start, most, axis=0)
    row_cand = jnp.arange(most * CAP, dtype=jnp.int32) // CAP
    owned = image_of(cand_counts, start + row_cand) == group
    live = wide(jnp.arange(most * CAP, dtype=jnp.int32) % CAP) < jnp.repeat(lengths, CAP)
    own_allowed = (row_cand[:, None] == row_cand[None, :]) & live[None, :]
    image_kv = image_kv.reshape(rows, 2, share // DH, DH)
    query = near[:, 0]

    def scores_of(keys):
        return jnp.einsum(
            "qhd,khd->hqk", query, keys, preferred_element_type=jnp.float32
        ) * DH ** (-0.5)

    def mixed(weights, values):
        return jnp.einsum(
            "hqk,khd->hqd", slim(weights), values, preferred_element_type=jnp.float32
        )

    image_scores = scores_of(image_kv[:, 0])
    own_scores = jnp.where(own_allowed[None], scores_of(near[:, 1]), FLOOR)
    top = jnp.maximum(
        jnp.max(image_scores, axis=-1, keepdims=True), jnp.max(own_scores, axis=-1, keepdims=True)
    )
    image_weights = jnp.exp(image_scores - top)
    own_weights = jnp.where(own_allowed[None], jnp.exp(own_scores - top), 0.0)
    total = jnp.sum(image_weights, axis=-1, keepdims=True) + jnp.sum(
        own_weights, axis=-1, keepdims=True
    )
    result = (mixed(image_weights, image_kv[:, 1]) + mixed(own_weights, near[:, 2])) / total
    result = jnp.where(owned[:, None, None], slim(result).transpose(1, 0, 2), 0)
    spread_out = lax.dynamic_update_slice_in_dim(
        jnp.zeros((cands * CAP, share), jnp.bfloat16),
        result.reshape(most * CAP, share),
        start * CAP,
        axis=0,
    )
    attended = lax.psum_scatter(spread_out, "grp", scatter_dimension=0, tiled=True)
    if shares > 1:
        attended = joined(attended, "vis", 1)
    partial_words = dot(attended, out_weight).reshape(cand_local, CAP, out_weight.shape[1])
    words_out = lax.psum_scatter(partial_words, "enc", scatter_dimension=1, tiled=True)
    caption_out = slim(words + words_out)
    return (vision_rows[None], caption_out)


def solution(mesh):
    return jax.shard_map(
        on_device,
        mesh=mesh,
        in_specs=(
            P("grp", None, "enc"),
            P("enc"),
            P("enc", ("vis", "grp")),
            P(("vis", "grp"), "enc"),
            P("enc", "vis"),
            P("vis"),
            P(None, "vis", "enc"),
            P("enc", "vis"),
            P("grp", "enc", "vis"),
            P(),
            P("grp"),
        ),
        out_specs=(P("grp", None, "enc"), P("grp", "enc", "vis")),
        check_vma=False,
    )
```

time: 1200 us -> 414 us (0.34)
  waiting for transfers between devices: 1040 us -> 187 us
  starting transfers between devices: 0.55 us -> 62.5 us
    all_gather x3 -> x1, waiting for transfers between devices: 695 us -> 0.01 us  [on_device(): every_word = lax.all_gather(word_qkv, 'grp', axis=0, tiled=True)]
    psum x3 -> x0, waiting for transfers between devices: 303 us -> none  [the longest x1 155 us: on_device(): lax.psum(partial_pre, 'enc')]
    ppermute x0 -> x35, waiting for transfers between devices: none -> 131 us  [the longest x27 70.6 us: shifted(): lax.ppermute(value, axis, [(i, (i + step) % count) for i in range(count)])]
    ppermute x0 -> x35, starting transfers between devices: none -> 62.2 us  [the longest x6 34.8 us: to_place(): lax.ppermute(value, 'grp', [(i, (i + step * cores) % groups) for i in ran...]
    unnamed x0 -> x1, blocking collectives: none -> 18.5 us
    all_gather x3 -> x0, blocking collectives: 16.5 us -> none  [the longest x1 5.91 us: on_device(): own_rows = lax.all_gather(projected[:, 1:], 'vis', axis=0, tiled=True)]
    another operation x5 -> x0, local copies, waits for them, and re-layouts: 15.9 us -> none  [the longest x2 7.92 us: softmax_update(): value_heads = values.reshape(count, heads, width)]
    dot_general x10 -> x29, matrix products: 83.2 us -> 93.6 us  [the longest x19 77.4 us: dot(): return jnp.dot(a, b, preferred_element_type=jnp.float32)]
  transfers between devices with their start and end apart: 9 -> 38, of which waited for: 9 -> 17; matrix products, arithmetic and copies ran while one was open for 3% -> 26% of each run, Pallas kernels for 0% -> 0%
where the time goes in v1:
time: 414 us; the launch traced here: 409 us
  waiting for transfers between devices  187 us (45%)
  matrix products  93.6 us (23%)
  starting transfers between devices  62.5 us (15%)
  other arithmetic  19.6 us (5%)
  blocking collectives  18.5 us (4%)
  between operations  16.8 us (4%)
  local copies, waits for them, and re-layouts  11.2 us (3%)
    dot_general x19, matrix products, dot(): return jnp.dot(a, b, preferred_element_type=jnp.float32)  77.4 us
    ppermute x27, waiting for transfers between devices, shifted(): lax.ppermute(value, axis, [(i, (i + step) % count) for i in range(count)])  70.6 us
    ppermute x6, waiting for transfers between devices, to_place(): lax.ppermute(value, 'grp', [(i, (i + step * cores) % groups) for i in ran...  60.9 us
    reduce_scatter x1, waiting for transfers between devices, on_device(): lax.psum_scatter(spread_out, 'grp', scatter_dimension=0, tiled=True)  43.8 us
    ppermute x6, starting transfers between devices, to_place(): lax.ppermute(value, 'grp', [(i, (i + step * cores) % groups) for i in ran...  34.8 us
    ppermute x27, starting transfers between devices, shifted(): lax.ppermute(value, axis, [(i, (i + step) % count) for i in range(count)])  26.9 us
    unnamed x1, blocking collectives  18.5 us
    reduce_scatter x1, waiting for transfers between devices, on_device(): lax.psum_scatter(partial_words, 'enc', scatter_dimension=1, tiled=True)  11.4 us
  transfers between devices with their start and end apart: 38, of which 17 were waited for; matrix products, arithmetic and copies ran while one was open for 26% of the time, Pallas kernels for 0%

profile of v1, /device:TPU:0, one launch (start us, length us, event | category | flops | bytes accessed | tf_op | source)
XLA Modules:
  0.0 409.0 jit_solution(3980516290865997394)
XLA Ops:
  10.9 3.0 collective-permute-start
  20.8 18.5 %all-reduce = f32[32]{0:T(128)S(1)} all-reduce(f32[32]{0:T(128)S(1)} %convert_dynamic-update-slice_fusion), channel_id=1, replica_groups=mesh['vis'=2,'grp'=8,'enc'=2] {'grp'}, use_global_device_ids=true, to_apply=%add | all-reduce | flops 32 | bytes 256
  49.1 7.6 %collective-permute-done.1 = bf16[256,768]{1,0:T(8,128)(2,1)} collective-permute-done((bf16[256,768]{1,0:T(8,128)(2,1)}, bf16[256,768]{1,0:T(8,128)(2,1)}, u32[]{:S(2)}, u32[]{:S(2)}) %collective-permute-start.1) | collective-permute-done | bytes 393248 | tf_op jit(solution)/shard_map/ppermute | solution.py:34
  59.2 5.8 %fusion.135 = f32[256,3072]{1,0:T(8,128)S(1)} fusion(bf16[768,3072]{1,0:T(8,128)(2,1)} %param.14, f32[256,768]{1,0:T(8,128)} %get-tuple-element.22, bf16[256,768]{1,0:T(8,128)(2,1)} %collective-permute-done.1), kind=kOutput, calls=%fused_computation.233 | convolution fusion | flops 1221132288 | bytes 9043968 | tf_op jit(solution)/shard_map/dot_general | solution.py:21
  66.6 25.6 %collective-permute-done.12 = bf16[128,3072]{1,0:T(8,128)(2,1)S(1)} collective-permute-done((bf16[128,3072]{1,0:T(8,128)(2,1)S(1)}, bf16[128,3072]{1,0:T(8,128)(2,1)S(1)}, u32[]{:S(2)}, u32[]{:S(2)}) %collective-permute-start.12) | collective-permute-done | bytes 786464 | tf_op jit(solution)/shard_map/ppermute | solution.py:86
  96.5 16.1 %collective-permute-done.13 = bf16[128,3072]{1,0:T(8,128)(2,1)S(1)} collective-permute-done((bf16[128,3072]{1,0:T(8,128)(2,1)S(1)}, bf16[128,3072]{1,0:T(8,128)(2,1)S(1)}, u32[]{:S(2)}, u32[]{:S(2)}) %collective-permute-start.13) | collective-permute-done | bytes 786464 | tf_op jit(solution)/shard_map/ppermute | solution.py:34
  114.6 13.8 %collective-permute-done.19 = bf16[128,3072]{1,0:T(8,128)(2,1)S(1)} collective-permute-done((bf16[128,3072]{1,0:T(8,128)(2,1)S(1)}, bf16[128,3072]{1,0:T(8,128)(2,1)S(1)}, u32[]{:S(2)}, u32[]{:S(2)}) %collective-permute-start.19) | collective-permute-done | bytes 786464 | tf_op jit(solution)/shard_map/ppermute | solution.py:34
  133.6 3.2 fusion.131
  142.8 3.8 fusion.666
  147.3 3.8 fusion.664
  152.5 3.8 fusion.662
  157.0 3.7 fusion.660
  162.2 5.4 %convolution_add_fusion.2 = f32[256,3072]{1,0:T(8,128)S(1)} fusion(f32[256,3072]{1,0:T(8,128)S(1)} %fusion.133, bf16[768,3072]{1,0:T(8,128)(2,1)} %collective-permute-done.4, f32[256,768]{1,0:T(8,128)S(1)} %get-tuple-element.36, bf16[256,768]{1,0:T(8,128)(2,1)S(1)} %collective-permute-done.9), kind=kOutput, calls=%fused_computation.6 | convolution fusion | flops 1221918720 | bytes 12189696 | tf_op jit(solution)/shard_map/dot_general | solution.py:21
  169.3 5.6 %convolution_add_fusion.1 = f32[256,3072]{1,0:T(8,128)S(1)} fusion(f32[256,3072]{1,0:T(8,128)S(1)} %fusion.131, bf16[768,3072]{1,0:T(8,128)(2,1)} %collective-permute-done.4, f32[256,768]{1,0:T(8,128)S(1)} %get-tuple-element.32, bf16[256,768]{1,0:T(8,128)(2,1)S(1)} %collective-permute-done.15), kind=kOutput, calls=%fused_computation.5 | convolution fusion | flops 1221918720 | bytes 12189696 | tf_op jit(solution)/shard_map/dot_general | solution.py:21
  175.6 5.6 %convolution_add_fusion = f32[256,3072]{1,0:T(8,128)S(1)} fusion(f32[256,3072]{1,0:T(8,128)S(1)} %fusion.129, bf16[768,3072]{1,0:T(8,128)(2,1)} %collective-permute-done.4, f32[256,768]{1,0:T(8,128)S(1)} %get-tuple-element.28, bf16[256,768]{1,0:T(8,128)(2,1)S(1)} %collective-permute-done.21), kind=kOutput, calls=%fused_computation.4 | convolution fusion | flops 1221918720 | bytes 12189696 | tf_op jit(solution)/shard_map/dot_general | solution.py:21
  182.8 5.6 %convolution_add_fusion.3 = f32[256,3072]{1,0:T(8,128)S(1)} fusion(f32[256,3072]{1,0:T(8,128)S(1)} %fusion.135, bf16[768,3072]{1,0:T(8,128)(2,1)} %collective-permute-done.4, f32[256,768]{1,0:T(8,128)S(1)} %get-tuple-element.24, bf16[256,768]{1,0:T(8,128)(2,1)S(1)} %collective-permute-done.3), kind=kOutput, calls=%fused_computation.7 | convolution fusion | flops 1221918720 | bytes 12189696 | tf_op jit(solution)/shard_map/dot_general | solution.py:21
  190.2 14.6 %collective-permute-start.11 = (bf16[128,3072]{1,0:T(8,128)(2,1)}, bf16[128,3072]{1,0:T(8,128)(2,1)S(1)}, u32[]{:S(2)}, u32[]{:S(2)}) collective-permute-start(bf16[128,3072]{1,0:T(8,128)(2,1)} %fusion.18), channel_id=1, source_target_pairs={{0,12},{2,14},{4,0},{6,2},{8,4},{10,6},{12,8},{14,10},{1,13},{3,15... | collective-permute-start | bytes 2359304 | tf_op jit(solution)/shard_map/ppermute | solution.py:86
  206.1 5.8 %collective-permute-start.17 = (bf16[128,3072]{1,0:T(8,128)(2,1)}, bf16[128,3072]{1,0:T(8,128)(2,1)S(1)}, u32[]{:S(2)}, u32[]{:S(2)}) collective-permute-start(bf16[128,3072]{1,0:T(8,128)(2,1)} %fusion.17), channel_id=1, source_target_pairs={{0,8},{2,10},{4,12},{6,14},{8,0},{10,2},{12,4},{14,6},{1,9},{3,11}... | collective-permute-start | bytes 2359304 | tf_op jit(solution)/shard_map/ppermute | solution.py:86
  211.9 10.0 %collective-permute-done.22 = bf16[128,3072]{1,0:T(8,128)(2,1)S(1)} collective-permute-done((bf16[128,3072]{1,0:T(8,128)(2,1)S(1)}, bf16[128,3072]{1,0:T(8,128)(2,1)S(1)}, u32[]{:S(2)}, u32[]{:S(2)}) %collective-permute-start.22) | collective-permute-done | bytes 786464 | tf_op jit(solution)/shard_map/ppermute | solution.py:34
  223.0 11.8 %collective-permute-start.23 = (bf16[128,3072]{1,0:T(8,128)(2,1)}, bf16[128,3072]{1,0:T(8,128)(2,1)}, u32[]{:S(2)}, u32[]{:S(2)}) collective-permute-start(bf16[128,3072]{1,0:T(8,128)(2,1)} %fusion.16), channel_id=1, source_target_pairs={{0,4},{2,6},{4,8},{6,10},{8,12},{10,14},{12,0},{14,2},{1,5},{3,7},... | collective-permute-start | bytes 2359304 | tf_op jit(solution)/shard_map/ppermute | solution.py:86
  237.6 4.1 %collective-permute-done.27 = bf16[64,3,512]{2,0,1:T(8,128)(2,1)S(1)} collective-permute-done((bf16[64,3,512]{2,0,1:T(8,128)(2,1)S(1)}, bf16[64,3,512]{2,0,1:T(8,128)(2,1)S(1)}, u32[]{:S(2)}, u32[]{:S(2)}) %collective-permute-start.27) | collective-permute-done | bytes 196640 | tf_op jit(solution)/shard_map/ppermute | solution.py:34
  244.1 35.3 %collective-permute-done.17 = bf16[128,3072]{1,0:T(8,128)(2,1)S(1)} collective-permute-done((bf16[128,3072]{1,0:T(8,128)(2,1)}, bf16[128,3072]{1,0:T(8,128)(2,1)S(1)}, u32[]{:S(2)}, u32[]{:S(2)}) %collective-permute-start.17) | collective-permute-done | bytes 786464 | tf_op jit(solution)/shard_map/ppermute | solution.py:86
  282.9 7.2 %fusion.667 = (bf16[128,2048]{1,0:T(8,128)(2,1)}, f32[128,2048]{1,0:T(8,128)S(1)}) fusion(bf16[128,3072]{1,0:T(8,128)(2,1)S(1)} %fusion.23, bf16[3072,2048]{1,0:T(8,128)(2,1)} %param.15), kind=kOutput, calls=%fused_computation.797 | convolution fusion | flops 1610874880 | bytes 14942208 | tf_op jit(solution)/shard_map/dot_general | solution.py:21
  290.1 4.1 %collective-permute-done.24 = bf16[128,3072]{1,0:T(8,128)(2,1)S(1)} collective-permute-done((bf16[128,3072]{1,0:T(8,128)(2,1)S(1)}, bf16[128,3072]{1,0:T(8,128)(2,1)S(1)}, u32[]{:S(2)}, u32[]{:S(2)}) %collective-permute-start.24) | collective-permute-done | bytes 786464 | tf_op jit(solution)/shard_map/ppermute | solution.py:34
  294.2 7.5 %fusion.668 = (bf16[128,2048]{1,0:T(8,128)(2,1)}, f32[128,2048]{1,0:T(8,128)}) fusion(bf16[128,3072]{1,0:T(8,128)(2,1)S(1)} %collective-permute-done.24, bf16[3072,2048]{1,0:T(8,128)(2,1)} %param.15), kind=kOutput, calls=%fused_computation.798 | convolution fusion | flops 1610874880 | bytes 14942208 | tf_op jit(solution)/shard_map/dot_general | solution.py:21
  307.0 4.2 %collective-permute-done.29 = bf16[128,2048]{1,0:T(8,128)(2,1)} collective-permute-done((bf16[128,2048]{1,0:T(8,128)(2,1)}, bf16[128,2048]{1,0:T(8,128)(2,1)}, u32[]{:S(2)}, u32[]{:S(2)}) %collective-permute-start.29) | collective-permute-done | bytes 524320 | tf_op jit(solution)/shard_map/ppermute | solution.py:34
  314.0 3.1 fusion.24
  319.1 3.1 fusion.27
  334.4 43.8 %reduce-scatter.3.cloned.1.call-done = bf16[64,512]{1,0:T(8,128)(2,1)} async-done(((bf16[512,512]{1,0:T(8,128)(2,1)}), bf16[64,512]{1,0:T(8,128)(2,1)}) %reduce-scatter.3.cloned.1.call-update) | async-done | bytes 65552 | tf_op jit(solution)/shard_map/reduce_scatter | solution.py:273
  379.7 3.0 collective-permute-done.34
  383.6 3.9 fusion.394
  389.0 11.4 %reduce-scatter.5.cloned.1.call-done = f32[4,8,2048]{2,1,0:T(8,128)} async-done(((f32[4,16,2048]{2,1,0:T(8,128)}), f32[4,8,2048]{2,1,0:T(8,128)}) %reduce-scatter.5.cloned.1.call-update) | async-done | bytes 262160 | tf_op jit(solution)/shard_map/reduce_scatter | solution.py:277
  (184 shorter events, 88.6 us)
Async XLA Ops:
  7.2 294.6 %all-gather.2.cloned.1.call-start = ((), (), s32[]{:S(2)}) async-start(), calls=%async_computation.2 | async-start | bytes 1769472 | tf_op jit(solution)/shard_map/all_gather | solution.py:190
  10.9 28.6 %collective-permute-start = (f32[2,256]{1,0:T(2,128)S(1)}, f32[2,256]{1,0:T(2,128)S(1)}, u32[]{:S(2)}, u32[]{:S(2)}) collective-permute-start(f32[2,256]{1,0:T(2,128)S(1)} %pad_maximum_fusion.4), channel_id=1, source_target_pairs={{0,1},{1,0},{2,3},{3,2},{4,5},{5,4},{6,7},{7,6},{8,9},{9,8},{10,11... | collective-permute-start | bytes 6152 | tf_op jit(solution)/shard_map/ppermute | solution.py:34
  13.9 128.8 %collective-permute-start.2 = (bf16[3072,768]{1,0:T(8,128)(2,1)}, bf16[3072,768]{1,0:T(8,128)(2,1)}, u32[]{:S(2)}, u32[]{:S(2)}) collective-permute-start(bf16[3072,768]{1,0:T(8,128)(2,1)} %param.13), channel_id=1, source_target_pairs={{0,2},{2,0},{4,6},{6,4},{8,10},{10,8},{12,14},{14,12},{1,3},{3,1},... | collective-permute-start | bytes 14155784 | tf_op jit(solution)/shard_map/ppermute | solution.py:82
  13.9 148.2 %collective-permute-start.4 = (bf16[768,3072]{1,0:T(8,128)(2,1)}, bf16[768,3072]{1,0:T(8,128)(2,1)}, u32[]{:S(2)}, u32[]{:S(2)}) collective-permute-start(bf16[768,3072]{1,0:T(8,128)(2,1)} %param.14), channel_id=1, source_target_pairs={{0,2},{2,0},{4,6},{6,4},{8,10},{10,8},{12,14},{14,12},{1,3},{3,1},... | collective-permute-start | bytes 14155784 | tf_op jit(solution)/shard_map/ppermute | solution.py:83
  14.4 30.2 %collective-permute-start.25 = (bf16[4,8,2048]{2,1,0:T(8,128)(2,1)S(1)}, bf16[4,8,2048]{2,1,0:T(8,128)(2,1)S(1)}, u32[]{:S(2)}, u32[]{:S(2)}) collective-permute-start(bf16[4,8,2048]{2,1,0:T(8,128)(2,1)S(1)} %copy-done.5), channel_id=1, source_target_pairs={{0,1},{1,0},{2,3},{3,2},{4,5},{5,4},{6,7},{7,6},{8,9},{9,8},{10,11... | collective-permute-start | bytes 393224 | tf_op jit(solution)/shard_map/ppermute | solution.py:34
  40.4 24.6 %collective-permute-start.6 = (bf16[128,3072]{1,0:T(8,128)(2,1)S(1)}, bf16[128,3072]{1,0:T(8,128)(2,1)S(1)}, u32[]{:S(2)}, u32[]{:S(2)}) collective-permute-start(bf16[128,3072]{1,0:T(8,128)(2,1)S(1)} %get-tuple-element.6), channel_id=1, source_target_pairs={{0,4},{2,6},{4,8},{6,10},{8,12},{10,14},{12,0},{14,2},{1,5},{3,7},... | collective-permute-start | bytes 2359304 | tf_op jit(solution)/shard_map/ppermute | solution.py:86
  40.5 51.8 %collective-permute-start.12 = (bf16[128,3072]{1,0:T(8,128)(2,1)S(1)}, bf16[128,3072]{1,0:T(8,128)(2,1)S(1)}, u32[]{:S(2)}, u32[]{:S(2)}) collective-permute-start(bf16[128,3072]{1,0:T(8,128)(2,1)S(1)} %get-tuple-element.6), channel_id=1, source_target_pairs={{0,8},{2,10},{4,12},{6,14},{8,0},{10,2},{12,4},{14,6},{1,9},{3,11}... | collective-permute-start | bytes 2359304 | tf_op jit(solution)/shard_map/ppermute | solution.py:86
  48.4 8.3 %collective-permute-start.1 = (bf16[256,768]{1,0:T(8,128)(2,1)}, bf16[256,768]{1,0:T(8,128)(2,1)}, u32[]{:S(2)}, u32[]{:S(2)}) collective-permute-start(bf16[256,768]{1,0:T(8,128)(2,1)} %get-tuple-element.21), channel_id=1, source_target_pairs={{0,1},{1,0},{2,3},{3,2},{4,5},{5,4},{6,7},{7,6},{8,9},{9,8},{10,11... | collective-permute-start | bytes 1179656 | tf_op jit(solution)/shard_map/ppermute | solution.py:34
  56.7 37.0 %collective-permute-start.18 = (bf16[128,3072]{1,0:T(8,128)(2,1)S(1)}, bf16[128,3072]{1,0:T(8,128)(2,1)S(1)}, u32[]{:S(2)}, u32[]{:S(2)}) collective-permute-start(bf16[128,3072]{1,0:T(8,128)(2,1)S(1)} %get-tuple-element.6), channel_id=1, source_target_pairs={{0,12},{2,14},{4,0},{6,2},{8,4},{10,6},{12,8},{14,10},{1,13},{3,15... | collective-permute-start | bytes 2359304 | tf_op jit(solution)/shard_map/ppermute | solution.py:86
  65.0 29.4 %collective-permute-start.7 = (bf16[128,3072]{1,0:T(8,128)(2,1)S(1)}, bf16[128,3072]{1,0:T(8,128)(2,1)S(1)}, u32[]{:S(2)}, u32[]{:S(2)}) collective-permute-start(bf16[128,3072]{1,0:T(8,128)(2,1)S(1)} %collective-permute-done.6), channel_id=1, source_target_pairs={{0,16},{16,0},{1,17},{17,1},{2,18},{18,2},{3,19},{19,3},{4,20},{20... | collective-permute-start | bytes 2359304 | tf_op jit(solution)/shard_map/ppermute | solution.py:34
  92.2 20.4 %collective-permute-start.13 = (bf16[128,3072]{1,0:T(8,128)(2,1)S(1)}, bf16[128,3072]{1,0:T(8,128)(2,1)S(1)}, u32[]{:S(2)}, u32[]{:S(2)}) collective-permute-start(bf16[128,3072]{1,0:T(8,128)(2,1)S(1)} %collective-permute-done.12), channel_id=1, source_target_pairs={{0,16},{16,0},{1,17},{17,1},{2,18},{18,2},{3,19},{19,3},{4,20},{20... | collective-permute-start | bytes 2359304 | tf_op jit(solution)/shard_map/ppermute | solution.py:34
  93.7 34.6 %collective-permute-start.19 = (bf16[128,3072]{1,0:T(8,128)(2,1)S(1)}, bf16[128,3072]{1,0:T(8,128)(2,1)S(1)}, u32[]{:S(2)}, u32[]{:S(2)}) collective-permute-start(bf16[128,3072]{1,0:T(8,128)(2,1)S(1)} %collective-permute-done.18), channel_id=1, source_target_pairs={{0,16},{16,0},{1,17},{17,1},{2,18},{18,2},{3,19},{19,3},{4,20},{20... | collective-permute-start | bytes 2359304 | tf_op jit(solution)/shard_map/ppermute | solution.py:34
  96.0 34.4 %collective-permute-start.8 = (bf16[256,768]{1,0:T(8,128)(2,1)S(1)}, bf16[256,768]{1,0:T(8,128)(2,1)S(1)}, u32[]{:S(2)}, u32[]{:S(2)}) collective-permute-start(bf16[256,768]{1,0:T(8,128)(2,1)S(1)} %get-tuple-element.33), channel_id=1, source_target_pairs={{0,1},{1,0},{2,3},{3,2},{4,5},{5,4},{6,7},{7,6},{8,9},{9,8},{10,11... | collective-permute-start | bytes 1179656 | tf_op jit(solution)/shard_map/ppermute | solution.py:34
  114.1 19.5 %collective-permute-start.14 = (bf16[256,768]{1,0:T(8,128)(2,1)S(1)}, bf16[256,768]{1,0:T(8,128)(2,1)S(1)}, u32[]{:S(2)}, u32[]{:S(2)}) collective-permute-start(bf16[256,768]{1,0:T(8,128)(2,1)S(1)} %get-tuple-element.29), channel_id=1, source_target_pairs={{0,1},{1,0},{2,3},{3,2},{4,5},{5,4},{6,7},{7,6},{8,9},{9,8},{10,11... | collective-permute-start | bytes 1179656 | tf_op jit(solution)/shard_map/ppermute | solution.py:34
  129.8 10.0 %collective-permute-start.20 = (bf16[256,768]{1,0:T(8,128)(2,1)S(1)}, bf16[256,768]{1,0:T(8,128)(2,1)S(1)}, u32[]{:S(2)}, u32[]{:S(2)}) collective-permute-start(bf16[256,768]{1,0:T(8,128)(2,1)S(1)} %get-tuple-element.25), channel_id=1, source_target_pairs={{0,1},{1,0},{2,3},{3,2},{4,5},{5,4},{6,7},{7,6},{8,9},{9,8},{10,11... | collective-permute-start | bytes 1179656 | tf_op jit(solution)/shard_map/ppermute | solution.py:34
  146.6 15.6 %collective-permute-start.9 = (bf16[256,768]{1,0:T(8,128)(2,1)S(1)}, bf16[256,768]{1,0:T(8,128)(2,1)S(1)}, u32[]{:S(2)}, u32[]{:S(2)}) collective-permute-start(bf16[256,768]{1,0:T(8,128)(2,1)S(1)} %get-tuple-element.35), channel_id=1, source_target_pairs={{0,1},{1,0},{2,3},{3,2},{4,5},{5,4},{6,7},{7,6},{8,9},{9,8},{10,11... | collective-permute-start | bytes 1179656 | tf_op jit(solution)/shard_map/ppermute | solution.py:34
  151.1 18.2 %collective-permute-start.15 = (bf16[256,768]{1,0:T(8,128)(2,1)S(1)}, bf16[256,768]{1,0:T(8,128)(2,1)S(1)}, u32[]{:S(2)}, u32[]{:S(2)}) collective-permute-start(bf16[256,768]{1,0:T(8,128)(2,1)S(1)} %get-tuple-element.31), channel_id=1, source_target_pairs={{0,1},{1,0},{2,3},{3,2},{4,5},{5,4},{6,7},{7,6},{8,9},{9,8},{10,11... | collective-permute-start | bytes 1179656 | tf_op jit(solution)/shard_map/ppermute | solution.py:34
  156.3 19.3 %collective-permute-start.21 = (bf16[256,768]{1,0:T(8,128)(2,1)S(1)}, bf16[256,768]{1,0:T(8,128)(2,1)S(1)}, u32[]{:S(2)}, u32[]{:S(2)}) collective-permute-start(bf16[256,768]{1,0:T(8,128)(2,1)S(1)} %get-tuple-element.27), channel_id=1, source_target_pairs={{0,1},{1,0},{2,3},{3,2},{4,5},{5,4},{6,7},{7,6},{8,9},{9,8},{10,11... | collective-permute-start | bytes 1179656 | tf_op jit(solution)/shard_map/ppermute | solution.py:34
  160.7 22.1 %collective-permute-start.3 = (bf16[256,768]{1,0:T(8,128)(2,1)S(1)}, bf16[256,768]{1,0:T(8,128)(2,1)S(1)}, u32[]{:S(2)}, u32[]{:S(2)}) collective-permute-start(bf16[256,768]{1,0:T(8,128)(2,1)S(1)} %get-tuple-element.23), channel_id=1, source_target_pairs={{0,1},{1,0},{2,3},{3,2},{4,5},{5,4},{6,7},{7,6},{8,9},{9,8},{10,11... | collective-permute-start | bytes 1179656 | tf_op jit(solution)/shard_map/ppermute | solution.py:34
  167.7 21.4 %collective-permute-start.10 = (bf16[128,3072]{1,0:T(8,128)(2,1)S(1)}, bf16[128,3072]{1,0:T(8,128)(2,1)S(1)}, u32[]{:S(2)}, u32[]{:S(2)}) collective-permute-start(bf16[128,3072]{1,0:T(8,128)(2,1)S(1)} %slice.105), channel_id=1, source_target_pairs={{0,16},{16,0},{1,17},{17,1},{2,18},{18,2},{3,19},{19,3},{4,20},{20... | collective-permute-start | bytes 2359304 | tf_op jit(solution)/shard_map/ppermute | solution.py:34
  175.0 30.1 %collective-permute-start.16 = (bf16[128,3072]{1,0:T(8,128)(2,1)S(1)}, bf16[128,3072]{1,0:T(8,128)(2,1)S(1)}, u32[]{:S(2)}, u32[]{:S(2)}) collective-permute-start(bf16[128,3072]{1,0:T(8,128)(2,1)S(1)} %slice.104), channel_id=1, source_target_pairs={{0,16},{16,0},{1,17},{17,1},{2,18},{18,2},{3,19},{19,3},{4,20},{20... | collective-permute-start | bytes 2359304 | tf_op jit(solution)/shard_map/ppermute | solution.py:34
  181.3 40.7 %collective-permute-start.22 = (bf16[128,3072]{1,0:T(8,128)(2,1)S(1)}, bf16[128,3072]{1,0:T(8,128)(2,1)S(1)}, u32[]{:S(2)}, u32[]{:S(2)}) collective-permute-start(bf16[128,3072]{1,0:T(8,128)(2,1)S(1)} %slice.103), channel_id=1, source_target_pairs={{0,16},{16,0},{1,17},{17,1},{2,18},{18,2},{3,19},{19,3},{4,20},{20... | collective-permute-start | bytes 2359304 | tf_op jit(solution)/shard_map/ppermute | solution.py:34
  188.5 55.6 %collective-permute-start.5 = (bf16[128,3072]{1,0:T(8,128)(2,1)S(1)}, bf16[128,3072]{1,0:T(8,128)(2,1)S(1)}, u32[]{:S(2)}, u32[]{:S(2)}) collective-permute-start(bf16[128,3072]{1,0:T(8,128)(2,1)S(1)} %slice.106), channel_id=1, source_target_pairs={{0,16},{16,0},{1,17},{17,1},{2,18},{18,2},{3,19},{19,3},{4,20},{20... | collective-permute-start | bytes 2359304 | tf_op jit(solution)/shard_map/ppermute | solution.py:34
  190.2 53.9 %collective-permute-start.11 = (bf16[128,3072]{1,0:T(8,128)(2,1)}, bf16[128,3072]{1,0:T(8,128)(2,1)S(1)}, u32[]{:S(2)}, u32[]{:S(2)}) collective-permute-start(bf16[128,3072]{1,0:T(8,128)(2,1)} %fusion.18), channel_id=1, source_target_pairs={{0,12},{2,14},{4,0},{6,2},{8,4},{10,6},{12,8},{14,10},{1,13},{3,15... | collective-permute-start | bytes 2359304 | tf_op jit(solution)/shard_map/ppermute | solution.py:86
  206.1 73.3 %collective-permute-start.17 = (bf16[128,3072]{1,0:T(8,128)(2,1)}, bf16[128,3072]{1,0:T(8,128)(2,1)S(1)}, u32[]{:S(2)}, u32[]{:S(2)}) collective-permute-start(bf16[128,3072]{1,0:T(8,128)(2,1)} %fusion.17), channel_id=1, source_target_pairs={{0,8},{2,10},{4,12},{6,14},{8,0},{10,2},{12,4},{14,6},{1,9},{3,11}... | collective-permute-start | bytes 2359304 | tf_op jit(solution)/shard_map/ppermute | solution.py:86
  223.0 56.4 %collective-permute-start.23 = (bf16[128,3072]{1,0:T(8,128)(2,1)}, bf16[128,3072]{1,0:T(8,128)(2,1)}, u32[]{:S(2)}, u32[]{:S(2)}) collective-permute-start(bf16[128,3072]{1,0:T(8,128)(2,1)} %fusion.16), channel_id=1, source_target_pairs={{0,4},{2,6},{4,8},{6,10},{8,12},{10,14},{12,0},{14,2},{1,5},{3,7},... | collective-permute-start | bytes 2359304 | tf_op jit(solution)/shard_map/ppermute | solution.py:86
  243.7 134.6 %reduce-scatter.3.cloned.1.call-start = ((), (), s32[]{:S(2)}) async-start(), calls=%async_computation.3 | async-start | bytes 589824 | tf_op jit(solution)/shard_map/reduce_scatter | solution.py:273
  282.2 12.1 %collective-permute-start.24 = (bf16[128,3072]{1,0:T(8,128)(2,1)S(1)}, bf16[128,3072]{1,0:T(8,128)(2,1)S(1)}, u32[]{:S(2)}, u32[]{:S(2)}) collective-permute-start(bf16[128,3072]{1,0:T(8,128)(2,1)S(1)} %fusion.23), channel_id=1, source_target_pairs={{0,16},{16,0},{1,17},{17,1},{2,18},{18,2},{3,19},{19,3},{4,20},{20... | collective-permute-start | bytes 2359304 | tf_op jit(solution)/shard_map/ppermute | solution.py:34
  290.1 16.9 %collective-permute-start.28 = (bf16[128,2048]{1,0:T(8,128)(2,1)}, bf16[128,2048]{1,0:T(8,128)(2,1)}, u32[]{:S(2)}, u32[]{:S(2)}) collective-permute-start(bf16[128,2048]{1,0:T(8,128)(2,1)} %get-tuple-element.37), channel_id=1, source_target_pairs={{0,1},{1,0},{2,3},{3,2},{4,5},{5,4},{6,7},{7,6},{8,9},{9,8},{10,11... | collective-permute-start | bytes 1572872 | tf_op jit(solution)/shard_map/ppermute | solution.py:34
  301.8 9.5 %collective-permute-start.29 = (bf16[128,2048]{1,0:T(8,128)(2,1)}, bf16[128,2048]{1,0:T(8,128)(2,1)}, u32[]{:S(2)}, u32[]{:S(2)}) collective-permute-start(bf16[128,2048]{1,0:T(8,128)(2,1)} %get-tuple-element.39), channel_id=1, source_target_pairs={{0,1},{1,0},{2,3},{3,2},{4,5},{5,4},{6,7},{7,6},{8,9},{9,8},{10,11... | collective-permute-start | bytes 1572872 | tf_op jit(solution)/shard_map/ppermute | solution.py:34
  313.2 10.1 %collective-permute-start.31 = (f32[128]{0:T(128)S(1)}, f32[128]{0:T(128)S(1)}, u32[]{:S(2)}, u32[]{:S(2)}) collective-permute-start(f32[128]{0:T(128)S(1)} %get-tuple-element.17), channel_id=1, source_target_pairs={{0,16},{16,0},{1,17},{17,1},{2,18},{18,2},{3,19},{19,3},{4,20},{20... | collective-permute-start | bytes 1544 | tf_op jit(solution)/shard_map/ppermute | solution.py:34
  334.4 66.0 %reduce-scatter.5.cloned.1.call-start = ((), (), s32[]{:S(2)}) async-start(), calls=%async_computation.4 | async-start | bytes 786432 | tf_op jit(solution)/shard_map/reduce_scatter | solution.py:277
  (27 other events, 411.8 us)
Sparse Core Ops, SparseCore 0:
  243.8 36.4 all-gather.1
  334.5 43.7 reduce-scatter.2
  387.6 12.7 reduce-scatter.4

commit v2 on v1

--- a/solution.py
+++ b/solution.py
@@ -38,6 +38,10 @@
     if lax.axis_size(axis) != 2:
         return lax.psum(value, axis)
     return value + shifted(value, axis, 1)
+
+
+def ordered(value, first):
+    return lax.optimization_barrier((value, first))[0]
 
 
 def joined(value, axis, dim):
@@ -76,11 +80,12 @@
 
     cores = 2 if groups % 2 == 0 else 1
     places = groups // cores
+    place, core = group // cores, group % cores
+    core_swap = [(i, i ^ 1) for i in range(groups)]
     up_parts, down_parts = [up_weight], [down_weight]
     if cores == 2:
-        swap = [(i, i ^ 1) for i in range(groups)]
-        up_parts.append(lax.ppermute(up_weight, "grp", swap))
-        down_parts.append(lax.ppermute(down_weight, "grp", swap))
+        up_parts.append(lax.ppermute(up_weight, "grp", core_swap))
+        down_parts.append(lax.ppermute(down_weight, "grp", core_swap))
 
     def to_place(value, step):
         return lax.ppermute(
@@ -107,41 +112,54 @@
             return lax.psum_scatter(value, "vis", scatter_dimension=0, tiled=True)
         return value[:part_rows] + wide(shifted(slim(value[part_rows:]), "vis", 1))
 
+    my_tokens = mine_of(image_tokens[0])
+    my_blocks = {}
+    gate = my_tokens
+    for step in range(1, places):
+        my_blocks[step] = to_place(gate, step)
+        if step == 1:
+            gate = ordered(my_tokens, my_blocks[1])
+
     tokens = wide(image_tokens[0])
     row_total, row_squares = summed(
         jnp.stack([jnp.sum(tokens, axis=-1), jnp.sum(tokens * tokens, axis=-1)]), "enc"
     )
     mean = row_total / all_features
     spread = row_squares / all_features - mean * mean
-    normed = slim(
-        (tokens - mean[:, None]) * lax.rsqrt(spread + EPSILON)[:, None] * vision_gain
-    )
-    my_normed = mine_of(normed)
+    stats = jnp.stack([mean, lax.rsqrt(spread + EPSILON)])
+
+    def normalized(block, step):
+        moved = by_halves(jnp.transpose(to_place(stats, step) if step else stats))
+        return slim((wide(block) - moved[:, :1]) * moved[:, 1:] * vision_gain)
 
     def pre_of(block):
-        return [dot(block, weight) for weight in up_parts]
+        return jnp.concatenate([dot(block, weight) for weight in up_parts], axis=1)
 
     def out_of(pre):
-        total = None
-        for part, weight in zip(pre, down_parts):
-            if enc_count == 2:
-                full = part + wide(shifted(slim(part), "enc", 1))
-            else:
-                full = lax.psum(part, "enc")
-            term = dot(slim(jax.nn.gelu(full, approximate=False)), weight)
-            total = term if total is None else total + term
-        return total
-
-    order = [0] + list(range(1, places))
-    my_out = None
-    blocks = [by_halves(normed)]
-    blocks += [all_rows(to_place(my_normed, step)) for step in order[1:]]
-    for step, block in zip(order, blocks):
-        partial = my_rows_sum(out_of(pre_of(block)))
+        if enc_count == 2:
+            full = pre + wide(shifted(slim(pre), "enc", 1))
+        else:
+            full = lax.psum(pre, "enc")
+        hidden = slim(jax.nn.gelu(full, approximate=False))
+        units = down_weight.shape[0]
+        terms = [
+            dot(hidden[:, at * units : (at + 1) * units], weight)
+            for at, weight in enumerate(down_parts)
+        ]
+        return sum(terms[1:], terms[0])
+
+    my_out = wide(my_tokens)
+    for step in range(places):
+        if step:
+            block = all_rows(my_blocks[step])
+            block = ordered(block, up_parts[-1])
+        else:
+            block = by_halves(image_tokens[0])
+        partial = my_rows_sum(out_of(pre_of(normalized(block, step))))
         if step:
             partial = wide(to_place(slim(partial), -step))
-        my_out = partial if my_out is None else my_out + partial
-    my_vision = slim(mine_of(tokens) + my_out)
+        my_out = my_out + partial
+    my_vision = slim(my_out)
 
     inner = qkv_weight.shape[2]
     heads = inner // DH
@@ -187,8 +205,22 @@
                 )
             )
         )
-    every_word = lax.all_gather(word_qkv, "grp", axis=0, tiled=True)
-    every_length = lax.all_gather(wide(caption_lengths), "grp", axis=0, tiled=True)
+    row_at = jnp.arange(word_rows, dtype=jnp.int32) % CAP
+    word_live = row_at < jnp.repeat(caption_lengths, CAP)
+    flags = jnp.broadcast_to(word_live[:, None].astype(jnp.bfloat16), (word_rows, 128))
+    message = jnp.concatenate([word_qkv.reshape(word_rows, 3 * share), flags], axis=1)
+    if cores == 2:
+        other = lax.ppermute(message, "grp", core_swap)
+        message = jnp.concatenate(
+            [jnp.where(core == 0, message, other), jnp.where(core == 0, other, message)]
+        )
+    place_rows = cores * word_rows
+    every_word = jnp.zeros((groups * word_rows, message.shape[1]), jnp.bfloat16)
+    for step in range(places):
+        moved = to_place(message, step) if step else message
+        every_word = lax.dynamic_update_slice_in_dim(
+            every_word, moved, (place - step) % places * place_rows, axis=0
+        )
 
     def embed(block):
         partial = dot(block, project_weight)
@@ -228,16 +260,15 @@
         power = lax.psum(power, "vis")
         image_kv = slim(total * lax.rsqrt(power / width + EPSILON)[:, None, None])
 
-    cands = every_length.shape[0]
+    cands = groups * cand_local
     most = min(MOSTC, cands)
     ends = jnp.cumsum(cand_counts)
     start = jnp.minimum(ends[group] - cand_counts[group], cands - most)
     near = lax.dynamic_slice_in_dim(every_word, start * CAP, most * CAP, axis=0)
-    near = near.reshape(most * CAP, 3, share // DH, DH)
-    lengths = lax.dynamic_slice_in_dim(every_length, start, most, axis=0)
+    live = near[:, 3 * share] > 0
+    near = near[:, : 3 * share].reshape(most * CAP, 3, share // DH, DH)
     row_cand = jnp.arange(most * CAP, dtype=jnp.int32) // CAP
     owned = image_of(cand_counts, start + row_cand) == group
-    live = wide(jnp.arange(most * CAP, dtype=jnp.int32) % CAP) < jnp.repeat(lengths, CAP)
     own_allowed = (row_cand[:, None] == row_cand[None, :]) & live[None, :]
     image_kv = image_kv.reshape(rows, 2, share // DH, DH)
     query = near[:, 0]
@@ -270,11 +301,51 @@
         start * CAP,
         axis=0,
     )
-    attended = lax.psum_scatter(spread_out, "grp", scatter_dimension=0, tiled=True)
-    if shares > 1:
-        attended = joined(attended, "vis", 1)
-    partial_words = dot(attended, out_weight).reshape(cand_local, CAP, out_weight.shape[1])
-    words_out = lax.psum_scatter(partial_words, "enc", scatter_dimension=1, tiled=True)
+    landed = None
+    for step in range(places):
+        part = lax.dynamic_slice_in_dim(
+            spread_out, (place + step) % places * place_rows, place_rows, axis=0
+        )
+        part = to_place(part, step) if step else part
+        landed = part if landed is None else landed + part
+    if cores == 2:
+        kept = lax.dynamic_slice_in_dim(landed, core * word_rows, word_rows, axis=0)
+        given = lax.dynamic_slice_in_dim(landed, (1 - core) * word_rows, word_rows, axis=0)
+        attended = kept + lax.ppermute(given, "grp", core_swap)
+    else:
+        kept, attended = landed, landed
+    if pair and shares == 2:
+        other = shifted(kept, "vis", 1)
+        if cores == 2:
+            across = [
+                (v * groups + i, (1 - v) * groups + (i ^ 1)) for v in range(2) for i in range(groups)
+            ]
+            other = other + lax.ppermute(given, ("vis", "grp"), across)
+        attended = jnp.concatenate([attended, other], axis=1)
+        final_weight = jnp.concatenate(
+            [
+                lax.dynamic_slice_in_dim(out_weight, vis * share, share, axis=0),
+                lax.dynamic_slice_in_dim(out_weight, (1 - vis) * share, share, axis=0),
+            ]
+        )
+    else:
+        if shares > 1:
+            attended = lax.all_gather(attended, "vis", axis=1, tiled=True)
+        final_weight = out_weight
+    if enc_count == 2:
+        enc = lax.axis_index("enc")
+        slots = CAP // enc_count
+        attended = attended.reshape(cand_local, CAP, inner)
+
+        def branch(which):
+            part = lax.dynamic_slice_in_dim(attended, which * slots, slots, axis=1)
+            return dot(part.reshape(cand_local * slots, inner), final_weight)
+
+        given = shifted(slim(branch(1 - enc)), "enc", 1)
+        words_out = (branch(enc) + wide(given)).reshape(words.shape)
+    else:
+        partial_words = dot(attended, final_weight).reshape(cand_local, CAP, out_weight.shape[1])
+        words_out = lax.psum_scatter(partial_words, "enc", scatter_dimension=1, tiled=True)
     caption_out = slim(words + words_out)
     return (vision_rows[None], caption_out)
 

time: 414 us -> 382 us (0.923)
  matrix products: 93.6 us -> 59.7 us
  starting transfers between devices: 62.5 us -> 88.2 us
  blocking collectives: 18.5 us -> 0 us
  waiting for transfers between devices: 187 us -> 171 us
  between operations: 16.8 us -> 2.96 us
  local copies, waits for them, and re-layouts: 11.2 us -> 24 us
  other arithmetic: 19.6 us -> 29.4 us
    reduce_scatter x2 -> x0, waiting for transfers between devices: 55.2 us -> none  [the longest x1 43.8 us: on_device(): lax.psum_scatter(spread_out, 'grp', scatter_dimension=0, tiled=True)]
    dot_general x19 -> x20, matrix products: 77.4 us -> 47.3 us  [dot(): return jnp.dot(a, b, preferred_element_type=jnp.float32)]
    ppermute x6 -> x15, starting transfers between devices: 34.8 us -> 58.8 us  [to_place(): lax.ppermute(value, 'grp', [(i, (i + step * cores) % groups) for i in ran...]
    ppermute x6 -> x15, waiting for transfers between devices: 60.9 us -> 81.5 us  [to_place(): lax.ppermute(value, 'grp', [(i, (i + step * cores) % groups) for i in ran...]
    ppermute x27 -> x24, waiting for transfers between devices: 70.6 us -> 89.4 us  [shifted(): lax.ppermute(value, axis, [(i, (i + step) % count) for i in range(count)])]
    unnamed x1 -> x0, blocking collectives: 18.5 us -> none
    convert_element_type x7 -> x13, other arithmetic: 8.39 us -> 20.9 us  [slim(): return a.astype(jnp.bfloat16)]
    ppermute x0 -> x3, local copies, waits for them, and re-layouts: none -> 5.98 us  [to_place(): lax.ppermute(value, 'grp', [(i, (i + step * cores) % groups) for i in ran...]
  transfers between devices with their start and end apart: 38 -> 44, of which waited for: 17 -> 24; matrix products, arithmetic and copies ran while one was open for 26% -> 27% of each run, Pallas kernels for 0% -> 0%
where the time goes in v2:
time: 382 us; the launch traced here: 375 us
  waiting for transfers between devices  171 us (45%)
  starting transfers between devices  88.2 us (23%)
  matrix products  59.7 us (16%)
  other arithmetic  29.4 us (8%)
  local copies, waits for them, and re-layouts  24 us (6%)
    ppermute x24, waiting for transfers between devices, shifted(): lax.ppermute(value, axis, [(i, (i + step) % count) for i in range(count)])  89.4 us
    ppermute x15, waiting for transfers between devices, to_place(): lax.ppermute(value, 'grp', [(i, (i + step * cores) % groups) for i in ran...  81.5 us
    ppermute x15, starting transfers between devices, to_place(): lax.ppermute(value, 'grp', [(i, (i + step * cores) % groups) for i in ran...  58.8 us
    dot_general x20, matrix products, dot(): return jnp.dot(a, b, preferred_element_type=jnp.float32)  47.3 us
    ppermute x24, starting transfers between devices, shifted(): lax.ppermute(value, axis, [(i, (i + step) % count) for i in range(count)])  27.9 us
    convert_element_type x13, other arithmetic, slim(): return a.astype(jnp.bfloat16)  20.9 us
  transfers between devices with their start and end apart: 44, of which 24 were waited for; matrix products, arithmetic and copies ran while one was open for 27% of the time, Pallas kernels for 0%

profile of v2, /device:TPU:0, one launch (start us, length us, event | category | flops | bytes accessed | tf_op | source)
XLA Modules:
  0.0 375.3 jit_solution(10426657728536786004)
XLA Ops:
  0.6 3.0 collective-permute-start.24
  14.3 3.9 %fusion.166 = f32[256,768]{1,0:T(8,128)S(1)} fusion(bf16[3072,768]{1,0:T(8,128)(2,1)} %param.13, bf16[128,3072]{1,0:T(8,128)(2,1)S(1)} %get-tuple-element.21, bf16[128,3072]{1,0:T(8,128)(2,1)S(1)} %get-tuple-element.7, f32[3072]{0:T(1024)S(1)} %copy-done.11, f32[256]{0:T(256)S(1)} %bitcast.161, f32[256]{0:T(256)S(1)} %bitcast.159), kind=kOutput, calls=%fused_computation.301 | convolution fusion | flops 1214251008 | bytes 7092224 | tf_op jit(solution)/shard_map/dot_general | solution.py:21
  18.1 9.3 %collective-permute-done.7 = f32[2,256]{1,0:T(2,128)S(1)} collective-permute-done((f32[2,256]{1,0:T(2,128)S(1)}, f32[2,256]{1,0:T(2,128)S(1)}, u32[]{:S(2)}, u32[]{:S(2)}) %collective-permute-start.7) | collective-permute-done | bytes 2080 | tf_op jit(solution)/shard_map/ppermute | solution.py:91
  33.2 4.1 %fusion.78 = bf16[64,3,512]{2,0,1:T(8,128)(2,1)S(1)} fusion(bf16[3,2048,1024]{2,1,0:T(8,128)(2,1)} %param.17, s32[]{:T(128)S(6)} %select_n.196, bf16[64,2048]{1,0:T(8,128)(2,1)S(1)} %fusion.86), kind=kOutput, calls=%fused_computation.144 | convolution fusion | flops 402751488 | bytes 6750212 | tf_op jit(solution)/shard_map/rd,kdh->rkh/dot_general | solution.py:190
  39.0 4.1 %collective-permute-done.26 = bf16[64,3,512]{2,0,1:T(8,128)(2,1)S(1)} collective-permute-done((bf16[64,3,512]{2,0,1:T(8,128)(2,1)S(1)}, bf16[64,3,512]{2,0,1:T(8,128)(2,1)S(1)}, u32[]{:S(2)}, u32[]{:S(2)}) %collective-permute-start.26) | collective-permute-done | bytes 196640 | tf_op jit(solution)/shard_map/ppermute | solution.py:34
  43.0 4.1 %fusion.111 = bf16[3,8,8,512]{3,2,1,0:T(8,128)(2,1)S(1)} fusion(bf16[64,3,512]{2,0,1:T(8,128)(2,1)S(1)} %collective-permute-done.26, bf16[3,2048,1024]{2,1,0:T(8,128)(2,1)} %param.17, s32[]{:T(128)S(6)} %select_n.195, bf16[64,2048]{1,0:T(8,128)(2,1)S(1)} %fusion.86), kind=kOutput, calls=%fused_computation.195 | convolution fusion | flops 402948096 | bytes 6946820 | tf_op jit(solution)/shard_map/rd,kdh->rkh/dot_general | solution.py:193
  49.7 23.1 %collective-permute-done.11 = bf16[128,3072]{1,0:T(8,128)(2,1)S(1)} collective-permute-done((bf16[128,3072]{1,0:T(8,128)(2,1)S(1)}, bf16[128,3072]{1,0:T(8,128)(2,1)S(1)}, u32[]{:S(2)}, u32[]{:S(2)}) %collective-permute-start.11) | collective-permute-done | bytes 786464 | tf_op jit(solution)/shard_map/ppermute | solution.py:91
  73.9 5.5 %collective-permute-done.17 = bf16[128,3072]{1,0:T(8,128)(2,1)S(1)} collective-permute-done((bf16[128,3072]{1,0:T(8,128)(2,1)S(1)}, bf16[128,3072]{1,0:T(8,128)(2,1)S(1)}, u32[]{:S(2)}, u32[]{:S(2)}) %collective-permute-start.17) | collective-permute-done | bytes 786464 | tf_op jit(solution)/shard_map/ppermute | solution.py:91
  81.5 10.3 %collective-permute-start.28 = (bf16[128,1664]{1,0:T(8,128)(2,1)}, bf16[128,1664]{1,0:T(8,128)(2,1)}, u32[]{:S(2)}, u32[]{:S(2)}) collective-permute-start(bf16[128,1664]{1,0:T(8,128)(2,1)} %pad_maximum_fusion.13), channel_id=1, source_target_pairs={{0,4},{2,6},{4,8},{6,10},{8,12},{10,14},{12,0},{14,2},{1,5},{3,7},... | collective-permute-start | bytes 1277960 | tf_op jit(solution)/shard_map/ppermute | solution.py:91
  95.2 13.8 %collective-permute-done.18 = bf16[128,3072]{1,0:T(8,128)(2,1)S(1)} collective-permute-done((bf16[128,3072]{1,0:T(8,128)(2,1)S(1)}, bf16[128,3072]{1,0:T(8,128)(2,1)S(1)}, u32[]{:S(2)}, u32[]{:S(2)}) %collective-permute-start.18) | collective-permute-done | bytes 786464 | tf_op jit(solution)/shard_map/ppermute | solution.py:34
  109.1 16.9 %collective-permute-start.30 = (bf16[128,1664]{1,0:T(8,128)(2,1)}, bf16[128,1664]{1,0:T(8,128)(2,1)}, u32[]{:S(2)}, u32[]{:S(2)}) collective-permute-start(bf16[128,1664]{1,0:T(8,128)(2,1)} %pad_maximum_fusion.13), channel_id=1, source_target_pairs={{0,12},{2,14},{4,0},{6,2},{8,4},{10,6},{12,8},{14,10},{1,13},{3,15... | collective-permute-start | bytes 1277960 | tf_op jit(solution)/shard_map/ppermute | solution.py:91
  127.6 3.9 %fusion.159 = f32[256,768]{1,0:T(8,128)S(1)} fusion(bf16[3072,768]{1,0:T(8,128)(2,1)} %collective-permute-done.1, bf16[256,3072]{1,0:T(8,128)(2,1)S(1)} %pad_maximum_fusion.6, f32[256]{0:T(256)S(1)} %bitcast.166, f32[256]{0:T(256)S(1)} %bitcast.164, f32[3072]{0:T(1024)S(1)} %copy-done.11), kind=kOutput, calls=%fused_computation.294 | convolution fusion | flops 1211891712 | bytes 7092224 | tf_op jit(solution)/shard_map/dot_general | solution.py:21
  134.4 3.9 %fusion.161 = f32[256,768]{1,0:T(8,128)S(1)} fusion(bf16[3072,768]{1,0:T(8,128)(2,1)} %collective-permute-done.1, bf16[256,3072]{1,0:T(8,128)(2,1)S(1)} %pad_maximum_fusion.8, f32[256]{0:T(256)S(1)} %bitcast.170, f32[256]{0:T(256)S(1)} %bitcast.168, f32[3072]{0:T(1024)S(1)} %copy-done.11), kind=kOutput, calls=%fused_computation.296 | convolution fusion | flops 1211891712 | bytes 7092224 | tf_op jit(solution)/shard_map/dot_general | solution.py:21
  139.8 3.9 %fusion.163 = f32[256,768]{1,0:T(8,128)S(1)} fusion(bf16[3072,768]{1,0:T(8,128)(2,1)} %collective-permute-done.1, bf16[256,3072]{1,0:T(8,128)(2,1)S(1)} %pad_maximum_fusion.10, f32[256]{0:T(256)S(1)} %bitcast.174, f32[256]{0:T(256)S(1)} %bitcast.172, f32[3072]{0:T(1024)S(1)} %copy-done.11), kind=kOutput, calls=%fused_computation.298 | convolution fusion | flops 1211891712 | bytes 7092224 | tf_op jit(solution)/shard_map/dot_general | solution.py:21
  143.8 3.8 %fusion.165 = f32[256,768]{1,0:T(8,128)S(1)} fusion(bf16[3072,768]{1,0:T(8,128)(2,1)} %collective-permute-done.1, bf16[128,3072]{1,0:T(8,128)(2,1)S(1)} %get-tuple-element.21, bf16[128,3072]{1,0:T(8,128)(2,1)S(1)} %get-tuple-element.7, f32[3072]{0:T(1024)S(1)} %copy-done.11, f32[256]{0:T(256)S(1)} %bitcast.162, f32[256]{0:T(256)S(1)} %bitcast.160), kind=kOutput, calls=%fused_computation.300 | convolution fusion | flops 1214251008 | bytes 7092224 | tf_op jit(solution)/shard_map/dot_general | solution.py:21
  150.6 3.7 fusion.21
  158.1 11.7 %collective-permute-done.14 = bf16[256,1536]{1,0:T(8,128)(2,1)S(1)} collective-permute-done((bf16[256,1536]{1,0:T(8,128)(2,1)S(1)}, bf16[256,1536]{1,0:T(8,128)(2,1)S(1)}, u32[]{:S(2)}, u32[]{:S(2)}) %collective-permute-start.14) | collective-permute-done | bytes 786464 | tf_op jit(solution)/shard_map/ppermute | solution.py:34
  171.0 3.5 fusion.24
  177.4 9.2 %collective-permute-done.20 = bf16[256,1536]{1,0:T(8,128)(2,1)S(1)} collective-permute-done((bf16[256,1536]{1,0:T(8,128)(2,1)S(1)}, bf16[256,1536]{1,0:T(8,128)(2,1)S(1)}, u32[]{:S(2)}, u32[]{:S(2)}) %collective-permute-start.20) | collective-permute-done | bytes 786464 | tf_op jit(solution)/shard_map/ppermute | solution.py:34
  187.3 3.9 %fusion.27 = bf16[256,1536]{1,0:T(8,128)(2,1)S(1)} fusion(bf16[256,1536]{1,0:T(8,128)(2,1)S(1)} %collective-permute-done.20, f32[256,768]{1,0:T(8,128)S(1)} %fusion.163, f32[256,768]{1,0:T(8,128)S(1)} %fusion.164), kind=kLoop, calls=%fused_computation.42 | loop fusion | flops 26738688 | bytes 3145728 | tf_op jit(solution)/shard_map/convert_element_type | solution.py:29
  194.0 5.6 %collective-permute-done.2 = bf16[256,1536]{1,0:T(8,128)(2,1)S(1)} collective-permute-done((bf16[256,1536]{1,0:T(8,128)(2,1)S(1)}, bf16[256,1536]{1,0:T(8,128)(2,1)S(1)}, u32[]{:S(2)}, u32[]{:S(2)}) %collective-permute-start.2) | collective-permute-done | bytes 786464 | tf_op jit(solution)/shard_map/ppermute | solution.py:34
  200.4 3.5 fusion.18
  210.1 10.0 %collective-permute-done.15 = bf16[128,3072]{1,0:T(8,128)(2,1)S(1)} collective-permute-done((bf16[128,3072]{1,0:T(8,128)(2,1)S(1)}, bf16[128,3072]{1,0:T(8,128)(2,1)S(1)}, u32[]{:S(2)}, u32[]{:S(2)}) %collective-permute-start.15) | collective-permute-done | bytes 786464 | tf_op jit(solution)/shard_map/ppermute | solution.py:34
  221.9 15.0 %collective-permute-done.21 = bf16[128,3072]{1,0:T(8,128)(2,1)S(1)} collective-permute-done((bf16[128,3072]{1,0:T(8,128)(2,1)S(1)}, bf16[128,3072]{1,0:T(8,128)(2,1)S(1)}, u32[]{:S(2)}, u32[]{:S(2)}) %collective-permute-start.21) | collective-permute-done | bytes 786464 | tf_op jit(solution)/shard_map/ppermute | solution.py:34
  255.6 39.7 %collective-permute-done.16 = bf16[128,3072]{1,0:T(8,128)(2,1)} collective-permute-done((bf16[128,3072]{1,0:T(8,128)(2,1)}, bf16[128,3072]{1,0:T(8,128)(2,1)}, u32[]{:S(2)}, u32[]{:S(2)}) %collective-permute-start.16) | collective-permute-done | bytes 786464 | tf_op jit(solution)/shard_map/ppermute | solution.py:91
  295.3 2.7 fusion.35
  300.4 6.5 %fusion.169 = (bf16[128,2048]{1,0:T(8,128)(2,1)S(1)}, f32[128,2048]{1,0:T(8,128)S(1)}) fusion(bf16[128,3072]{1,0:T(8,128)(2,1)S(1)} %fusion.35, bf16[3072,2048]{1,0:T(8,128)(2,1)} %param.15), kind=kOutput, calls=%fused_computation.304 | convolution fusion | flops 1610874880 | bytes 14942208 | tf_op jit(solution)/shard_map/dot_general | solution.py:21
  316.2 5.6 %collective-permute-done.32 = bf16[128,2048]{1,0:T(8,128)(2,1)S(1)} collective-permute-done((bf16[128,2048]{1,0:T(8,128)(2,1)S(1)}, bf16[128,2048]{1,0:T(8,128)(2,1)S(1)}, u32[]{:S(2)}, u32[]{:S(2)}) %collective-permute-start.32) | collective-permute-done | bytes 524320 | tf_op jit(solution)/shard_map/ppermute | solution.py:34
  328.0 2.9 collective-permute-done.36
  336.5 15.3 %collective-permute-start.37 = (bf16[128,512]{1,0:T(8,128)(2,1)S(1)}, bf16[128,512]{1,0:T(8,128)(2,1)S(1)}, u32[]{:S(2)}, u32[]{:S(2)}) collective-permute-start(bf16[128,512]{1,0:T(8,128)(2,1)S(1)} %get-tuple-element.22), channel_id=1, source_target_pairs={{0,4},{2,6},{4,8},{6,10},{8,12},{10,14},{12,0},{14,2},{1,5},{3,7},... | collective-permute-start | bytes 393224 | tf_op jit(solution)/shard_map/ppermute | solution.py:91
  353.8 2.8 collective-permute-start.39
  361.8 4.0 %constant_dynamic-slice_fusion.4 = (bf16[512,2048]{1,0:T(8,128)(2,1)S(1)}, bf16[512,2048]{1,0:T(8,128)(2,1)}) fusion(bf16[1024,2048]{1,0:T(8,128)(2,1)} %param.18, s32[]{:T(128)S(6)} %select_n.195, s32[]{:T(128)S(6)} %select_n.196), kind=kLoop, calls=%fused_computation.221 | loop fusion | bytes 8388616 | tf_op jit(solution)/shard_map/dynamic_slice | solution.py:327
  (222 shorter events, 113.1 us)
Async XLA Ops:
  0.6 28.5 %collective-permute-start.24 = (bf16[4,8,2048]{2,1,0:T(8,128)(2,1)}, bf16[4,8,2048]{2,1,0:T(8,128)(2,1)S(1)}, u32[]{:S(2)}, u32[]{:S(2)}) collective-permute-start(bf16[4,8,2048]{2,1,0:T(8,128)(2,1)} %param.19), channel_id=1, source_target_pairs={{0,1},{1,0},{2,3},{3,2},{4,5},{5,4},{6,7},{7,6},{8,9},{9,8},{10,11... | collective-permute-start | bytes 393224 | tf_op jit(solution)/shard_map/ppermute | solution.py:34
  6.0 32.8 %collective-permute-start.5 = (bf16[128,3072]{1,0:T(8,128)(2,1)S(1)}, bf16[128,3072]{1,0:T(8,128)(2,1)}, u32[]{:S(2)}, u32[]{:S(2)}) collective-permute-start(bf16[128,3072]{1,0:T(8,128)(2,1)S(1)} %get-tuple-element.7), channel_id=1, source_target_pairs={{0,4},{2,6},{4,8},{6,10},{8,12},{10,14},{12,0},{14,2},{1,5},{3,7},... | collective-permute-start | bytes 2359304 | tf_op jit(solution)/shard_map/ppermute | solution.py:91
  8.0 118.0 %collective-permute-start.1 = (bf16[3072,768]{1,0:T(8,128)(2,1)}, bf16[3072,768]{1,0:T(8,128)(2,1)}, u32[]{:S(2)}, u32[]{:S(2)}) collective-permute-start(bf16[3072,768]{1,0:T(8,128)(2,1)} %param.13), channel_id=1, source_target_pairs={{0,2},{2,0},{4,6},{6,4},{8,10},{10,8},{12,14},{14,12},{1,3},{3,1},... | collective-permute-start | bytes 14155784 | tf_op jit(solution)/shard_map/ppermute | solution.py:87
  11.0 16.4 %collective-permute-start.7 = (f32[2,256]{1,0:T(2,128)S(1)}, f32[2,256]{1,0:T(2,128)S(1)}, u32[]{:S(2)}, u32[]{:S(2)}) collective-permute-start(f32[2,256]{1,0:T(2,128)S(1)} %pad_maximum_fusion.18), channel_id=1, source_target_pairs={{0,4},{2,6},{4,8},{6,10},{8,12},{10,14},{12,0},{14,2},{1,5},{3,7},... | collective-permute-start | bytes 6152 | tf_op jit(solution)/shard_map/ppermute | solution.py:91
  12.7 26.2 %collective-permute-start.13 = (f32[2,256]{1,0:T(2,128)S(1)}, f32[2,256]{1,0:T(2,128)S(1)}, u32[]{:S(2)}, u32[]{:S(2)}) collective-permute-start(f32[2,256]{1,0:T(2,128)S(1)} %pad_maximum_fusion.18), channel_id=1, source_target_pairs={{0,8},{2,10},{4,12},{6,14},{8,0},{10,2},{12,4},{14,6},{1,9},{3,11}... | collective-permute-start | bytes 6152 | tf_op jit(solution)/shard_map/ppermute | solution.py:91
  27.4 20.5 %collective-permute-start.19 = (f32[2,256]{1,0:T(2,128)S(1)}, f32[2,256]{1,0:T(2,128)S(1)}, u32[]{:S(2)}, u32[]{:S(2)}) collective-permute-start(f32[2,256]{1,0:T(2,128)S(1)} %pad_maximum_fusion.18), channel_id=1, source_target_pairs={{0,12},{2,14},{4,0},{6,2},{8,4},{10,6},{12,8},{14,10},{1,13},{3,15... | collective-permute-start | bytes 6152 | tf_op jit(solution)/shard_map/ppermute | solution.py:91
  38.9 34.0 %collective-permute-start.11 = (bf16[128,3072]{1,0:T(8,128)(2,1)S(1)}, bf16[128,3072]{1,0:T(8,128)(2,1)S(1)}, u32[]{:S(2)}, u32[]{:S(2)}) collective-permute-start(bf16[128,3072]{1,0:T(8,128)(2,1)S(1)} %get-tuple-element.7), channel_id=1, source_target_pairs={{0,8},{2,10},{4,12},{6,14},{8,0},{10,2},{12,4},{14,6},{1,9},{3,11}... | collective-permute-start | bytes 2359304 | tf_op jit(solution)/shard_map/ppermute | solution.py:91
  47.2 32.2 %collective-permute-start.17 = (bf16[128,3072]{1,0:T(8,128)(2,1)S(1)}, bf16[128,3072]{1,0:T(8,128)(2,1)S(1)}, u32[]{:S(2)}, u32[]{:S(2)}) collective-permute-start(bf16[128,3072]{1,0:T(8,128)(2,1)S(1)} %get-tuple-element.7), channel_id=1, source_target_pairs={{0,12},{2,14},{4,0},{6,2},{8,4},{10,6},{12,8},{14,10},{1,13},{3,15... | collective-permute-start | bytes 2359304 | tf_op jit(solution)/shard_map/ppermute | solution.py:91
  47.9 33.6 %collective-permute-start.6 = (bf16[128,3072]{1,0:T(8,128)(2,1)}, bf16[128,3072]{1,0:T(8,128)(2,1)S(1)}, u32[]{:S(2)}, u32[]{:S(2)}) collective-permute-start(bf16[128,3072]{1,0:T(8,128)(2,1)} %collective-permute-done.5), channel_id=1, source_target_pairs={{0,16},{16,0},{1,17},{17,1},{2,18},{18,2},{3,19},{19,3},{4,20},{20... | collective-permute-start | bytes 2359304 | tf_op jit(solution)/shard_map/ppermute | solution.py:34
  49.5 106.2 %collective-permute-start.3 = (bf16[768,3072]{1,0:T(8,128)(2,1)S(1)}, bf16[768,3072]{1,0:T(8,128)(2,1)S(1)}, u32[]{:S(2)}, u32[]{:S(2)}) collective-permute-start(bf16[768,3072]{1,0:T(8,128)(2,1)S(1)} %bitcast.179), channel_id=1, source_target_pairs={{0,2},{2,0},{4,6},{6,4},{8,10},{10,8},{12,14},{14,12},{1,3},{3,1},... | collective-permute-start | bytes 14155784 | tf_op jit(solution)/shard_map/ppermute | solution.py:88
  72.8 20.4 %collective-permute-start.12 = (bf16[128,3072]{1,0:T(8,128)(2,1)S(1)}, bf16[128,3072]{1,0:T(8,128)(2,1)S(1)}, u32[]{:S(2)}, u32[]{:S(2)}) collective-permute-start(bf16[128,3072]{1,0:T(8,128)(2,1)S(1)} %collective-permute-done.11), channel_id=1, source_target_pairs={{0,16},{16,0},{1,17},{17,1},{2,18},{18,2},{3,19},{19,3},{4,20},{20... | collective-permute-start | bytes 2359304 | tf_op jit(solution)/shard_map/ppermute | solution.py:34
  79.4 29.7 %collective-permute-start.18 = (bf16[128,3072]{1,0:T(8,128)(2,1)S(1)}, bf16[128,3072]{1,0:T(8,128)(2,1)S(1)}, u32[]{:S(2)}, u32[]{:S(2)}) collective-permute-start(bf16[128,3072]{1,0:T(8,128)(2,1)S(1)} %collective-permute-done.17), channel_id=1, source_target_pairs={{0,16},{16,0},{1,17},{17,1},{2,18},{18,2},{3,19},{19,3},{4,20},{20... | collective-permute-start | bytes 2359304 | tf_op jit(solution)/shard_map/ppermute | solution.py:34
  81.5 156.8 %collective-permute-start.28 = (bf16[128,1664]{1,0:T(8,128)(2,1)}, bf16[128,1664]{1,0:T(8,128)(2,1)}, u32[]{:S(2)}, u32[]{:S(2)}) collective-permute-start(bf16[128,1664]{1,0:T(8,128)(2,1)} %pad_maximum_fusion.13), channel_id=1, source_target_pairs={{0,4},{2,6},{4,8},{6,10},{8,12},{10,14},{12,0},{14,2},{1,5},{3,7},... | collective-permute-start | bytes 1277960 | tf_op jit(solution)/shard_map/ppermute | solution.py:91
  93.2 145.1 %collective-permute-start.29 = (bf16[128,1664]{1,0:T(8,128)(2,1)}, bf16[128,1664]{1,0:T(8,128)(2,1)}, u32[]{:S(2)}, u32[]{:S(2)}) collective-permute-start(bf16[128,1664]{1,0:T(8,128)(2,1)} %pad_maximum_fusion.13), channel_id=1, source_target_pairs={{0,8},{2,10},{4,12},{6,14},{8,0},{10,2},{12,4},{14,6},{1,9},{3,11}... | collective-permute-start | bytes 1277960 | tf_op jit(solution)/shard_map/ppermute | solution.py:91
  109.1 139.3 %collective-permute-start.30 = (bf16[128,1664]{1,0:T(8,128)(2,1)}, bf16[128,1664]{1,0:T(8,128)(2,1)}, u32[]{:S(2)}, u32[]{:S(2)}) collective-permute-start(bf16[128,1664]{1,0:T(8,128)(2,1)} %pad_maximum_fusion.13), channel_id=1, source_target_pairs={{0,12},{2,14},{4,0},{6,2},{8,4},{10,6},{12,8},{14,10},{1,13},{3,15... | collective-permute-start | bytes 1277960 | tf_op jit(solution)/shard_map/ppermute | solution.py:91
  131.6 17.8 %collective-permute-start.8 = (bf16[256,1536]{1,0:T(8,128)(2,1)S(1)}, bf16[256,1536]{1,0:T(8,128)(2,1)S(1)}, u32[]{:S(2)}, u32[]{:S(2)}) collective-permute-start(bf16[256,1536]{1,0:T(8,128)(2,1)S(1)} %fusion.66), channel_id=1, source_target_pairs={{0,1},{1,0},{2,3},{3,2},{4,5},{5,4},{6,7},{7,6},{8,9},{9,8},{10,11... | collective-permute-start | bytes 2359304 | tf_op jit(solution)/shard_map/ppermute | solution.py:34
  149.3 20.5 %collective-permute-start.14 = (bf16[256,1536]{1,0:T(8,128)(2,1)S(1)}, bf16[256,1536]{1,0:T(8,128)(2,1)S(1)}, u32[]{:S(2)}, u32[]{:S(2)}) collective-permute-start(bf16[256,1536]{1,0:T(8,128)(2,1)S(1)} %fusion.65), channel_id=1, source_target_pairs={{0,1},{1,0},{2,3},{3,2},{4,5},{5,4},{6,7},{7,6},{8,9},{9,8},{10,11... | collective-permute-start | bytes 2359304 | tf_op jit(solution)/shard_map/ppermute | solution.py:34
  155.7 31.0 %collective-permute-start.20 = (bf16[256,1536]{1,0:T(8,128)(2,1)S(1)}, bf16[256,1536]{1,0:T(8,128)(2,1)S(1)}, u32[]{:S(2)}, u32[]{:S(2)}) collective-permute-start(bf16[256,1536]{1,0:T(8,128)(2,1)S(1)} %fusion.64), channel_id=1, source_target_pairs={{0,1},{1,0},{2,3},{3,2},{4,5},{5,4},{6,7},{7,6},{8,9},{9,8},{10,11... | collective-permute-start | bytes 2359304 | tf_op jit(solution)/shard_map/ppermute | solution.py:34
  169.8 29.8 %collective-permute-start.2 = (bf16[256,1536]{1,0:T(8,128)(2,1)S(1)}, bf16[256,1536]{1,0:T(8,128)(2,1)S(1)}, u32[]{:S(2)}, u32[]{:S(2)}) collective-permute-start(bf16[256,1536]{1,0:T(8,128)(2,1)S(1)} %fusion.67), channel_id=1, source_target_pairs={{0,1},{1,0},{2,3},{3,2},{4,5},{5,4},{6,7},{7,6},{8,9},{9,8},{10,11... | collective-permute-start | bytes 2359304 | tf_op jit(solution)/shard_map/ppermute | solution.py:34
  186.7 21.1 %collective-permute-start.9 = (bf16[128,3072]{1,0:T(8,128)(2,1)S(1)}, bf16[128,3072]{1,0:T(8,128)(2,1)S(1)}, u32[]{:S(2)}, u32[]{:S(2)}) collective-permute-start(bf16[128,3072]{1,0:T(8,128)(2,1)S(1)} %slice.240), channel_id=1, source_target_pairs={{0,16},{16,0},{1,17},{17,1},{2,18},{18,2},{3,19},{19,3},{4,20},{20... | collective-permute-start | bytes 2359304 | tf_op jit(solution)/shard_map/ppermute | solution.py:34
  199.6 20.5 %collective-permute-start.15 = (bf16[128,3072]{1,0:T(8,128)(2,1)S(1)}, bf16[128,3072]{1,0:T(8,128)(2,1)S(1)}, u32[]{:S(2)}, u32[]{:S(2)}) collective-permute-start(bf16[128,3072]{1,0:T(8,128)(2,1)S(1)} %slice.239), channel_id=1, source_target_pairs={{0,16},{16,0},{1,17},{17,1},{2,18},{18,2},{3,19},{19,3},{4,20},{20... | collective-permute-start | bytes 2359304 | tf_op jit(solution)/shard_map/ppermute | solution.py:34
  207.8 29.2 %collective-permute-start.21 = (bf16[128,3072]{1,0:T(8,128)(2,1)S(1)}, bf16[128,3072]{1,0:T(8,128)(2,1)S(1)}, u32[]{:S(2)}, u32[]{:S(2)}) collective-permute-start(bf16[128,3072]{1,0:T(8,128)(2,1)S(1)} %slice.238), channel_id=1, source_target_pairs={{0,16},{16,0},{1,17},{17,1},{2,18},{18,2},{3,19},{19,3},{4,20},{20... | collective-permute-start | bytes 2359304 | tf_op jit(solution)/shard_map/ppermute | solution.py:34
  220.1 34.1 %collective-permute-start.4 = (bf16[128,3072]{1,0:T(8,128)(2,1)}, bf16[128,3072]{1,0:T(8,128)(2,1)}, u32[]{:S(2)}, u32[]{:S(2)}) collective-permute-start(bf16[128,3072]{1,0:T(8,128)(2,1)} %slice.241), channel_id=1, source_target_pairs={{0,16},{16,0},{1,17},{17,1},{2,18},{18,2},{3,19},{19,3},{4,20},{20... | collective-permute-start | bytes 2359304 | tf_op jit(solution)/shard_map/ppermute | solution.py:34
  237.0 18.6 %collective-permute-start.10 = (bf16[128,3072]{1,0:T(8,128)(2,1)}, bf16[128,3072]{1,0:T(8,128)(2,1)}, u32[]{:S(2)}, u32[]{:S(2)}) collective-permute-start(bf16[128,3072]{1,0:T(8,128)(2,1)} %fusion.30), channel_id=1, source_target_pairs={{0,12},{2,14},{4,0},{6,2},{8,4},{10,6},{12,8},{14,10},{1,13},{3,15... | collective-permute-start | bytes 2359304 | tf_op jit(solution)/shard_map/ppermute | solution.py:91
  238.3 57.0 %collective-permute-start.16 = (bf16[128,3072]{1,0:T(8,128)(2,1)}, bf16[128,3072]{1,0:T(8,128)(2,1)}, u32[]{:S(2)}, u32[]{:S(2)}) collective-permute-start(bf16[128,3072]{1,0:T(8,128)(2,1)} %fusion.29), channel_id=1, source_target_pairs={{0,8},{2,10},{4,12},{6,14},{8,0},{10,2},{12,4},{14,6},{1,9},{3,11}... | collective-permute-start | bytes 2359304 | tf_op jit(solution)/shard_map/ppermute | solution.py:91
  238.3 57.0 %collective-permute-start.22 = (bf16[128,3072]{1,0:T(8,128)(2,1)}, bf16[128,3072]{1,0:T(8,128)(2,1)}, u32[]{:S(2)}, u32[]{:S(2)}) collective-permute-start(bf16[128,3072]{1,0:T(8,128)(2,1)} %fusion.28), channel_id=1, source_target_pairs={{0,4},{2,6},{4,8},{6,10},{8,12},{10,14},{12,0},{14,2},{1,5},{3,7},... | collective-permute-start | bytes 2359304 | tf_op jit(solution)/shard_map/ppermute | solution.py:91
  298.0 12.1 %collective-permute-start.23 = (bf16[128,3072]{1,0:T(8,128)(2,1)S(1)}, bf16[128,3072]{1,0:T(8,128)(2,1)S(1)}, u32[]{:S(2)}, u32[]{:S(2)}) collective-permute-start(bf16[128,3072]{1,0:T(8,128)(2,1)S(1)} %fusion.35), channel_id=1, source_target_pairs={{0,16},{16,0},{1,17},{17,1},{2,18},{18,2},{3,19},{19,3},{4,20},{20... | collective-permute-start | bytes 2359304 | tf_op jit(solution)/shard_map/ppermute | solution.py:34
  306.9 9.2 %collective-permute-start.31 = (bf16[128,2048]{1,0:T(8,128)(2,1)S(1)}, bf16[128,2048]{1,0:T(8,128)(2,1)S(1)}, u32[]{:S(2)}, u32[]{:S(2)}) collective-permute-start(bf16[128,2048]{1,0:T(8,128)(2,1)S(1)} %get-tuple-element.51), channel_id=1, source_target_pairs={{0,1},{1,0},{2,3},{3,2},{4,5},{5,4},{6,7},{7,6},{8,9},{9,8},{10,11... | collective-permute-start | bytes 1572872 | tf_op jit(solution)/shard_map/ppermute | solution.py:34
  311.9 9.9 %collective-permute-start.32 = (bf16[128,2048]{1,0:T(8,128)(2,1)S(1)}, bf16[128,2048]{1,0:T(8,128)(2,1)S(1)}, u32[]{:S(2)}, u32[]{:S(2)}) collective-permute-start(bf16[128,2048]{1,0:T(8,128)(2,1)S(1)} %get-tuple-element.53), channel_id=1, source_target_pairs={{0,1},{1,0},{2,3},{3,2},{4,5},{5,4},{6,7},{7,6},{8,9},{9,8},{10,11... | collective-permute-start | bytes 1572872 | tf_op jit(solution)/shard_map/ppermute | solution.py:34
  324.5 6.5 %collective-permute-start.33 = (bf16[128,2,512]{2,0,1:T(8,128)(2,1)S(1)}, bf16[128,2,512]{2,0,1:T(8,128)(2,1)S(1)}, u32[]{:S(2)}, u32[]{:S(2)}) collective-permute-start(bf16[128,2,512]{2,0,1:T(8,128)(2,1)S(1)} %fusion.68), channel_id=1, source_target_pairs={{0,16},{16,0},{1,17},{17,1},{2,18},{18,2},{3,19},{19,3},{4,20},{20... | collective-permute-start | bytes 786440 | tf_op jit(solution)/shard_map/ppermute | solution.py:34
  327.3 6.4 %collective-permute-start.35 = (bf16[128,2,512]{2,0,1:T(8,128)(2,1)S(1)}, bf16[128,2,512]{2,0,1:T(8,128)(2,1)S(1)}, u32[]{:S(2)}, u32[]{:S(2)}) collective-permute-start(bf16[128,2,512]{2,0,1:T(8,128)(2,1)S(1)} %fusion.71), channel_id=1, source_target_pairs={{0,16},{16,0},{1,17},{17,1},{2,18},{18,2},{3,19},{19,3},{4,20},{20... | collective-permute-start | bytes 786440 | tf_op jit(solution)/shard_map/ppermute | solution.py:34
  336.5 20.1 %collective-permute-start.37 = (bf16[128,512]{1,0:T(8,128)(2,1)S(1)}, bf16[128,512]{1,0:T(8,128)(2,1)S(1)}, u32[]{:S(2)}, u32[]{:S(2)}) collective-permute-start(bf16[128,512]{1,0:T(8,128)(2,1)S(1)} %get-tuple-element.22), channel_id=1, source_target_pairs={{0,4},{2,6},{4,8},{6,10},{8,12},{10,14},{12,0},{14,2},{1,5},{3,7},... | collective-permute-start | bytes 393224 | tf_op jit(solution)/shard_map/ppermute | solution.py:91
  (35 other events, 603.6 us)
